TPU v7x, 32 devices: a whole 2x2x4 slice. The times are simulated.
32 devices in a mesh: az: 16 (over z, y, x), rad: 2 (over core).
Axes of the slice: x: 2, y: 2, z: 4, core: 2. Of those that a mesh axis runs over, the one named last changes fastest.
Arguments:
- fields: float32 [5, 2, 192, 4096], P(None, None, 'rad', 'az'), as said below
- shifts: int32 [192], P('rad'), may hold values from 0 to 4095, as said below
- cycle_area: float32 [192], P('rad'), may hold values from 0.5 to 2
- gravity: float32 [192], P('rad'), may hold values from 0.00052083336 to 0.0052083335
- kappa_az: float32 [192], P('rad'), may hold values from 0.05 to 0.24
- kappa_rad: float32 [192], P('rad'), may hold values from 0.05 to 0.24
Outputs:
- updated: float32 [5, 2, 192, 4096], P(None, None, 'rad', 'az')
- enclosed: float32 [192], P('rad')
Inputs may be any that keep to these rules, and one draw needn't show every extreme that they name: shifts[r] is the whole number of cells by which row r moves toward higher azimuth. fields[0] is positive.
All inputs are finite; a program needn't handle non-finite values.
Results may differ from a plain program's by a relative error of at most 0.00002.
Values sent between devices are 32-bit elements; how exact they have to be, the bound alone decides.
A program may use at most 64 MiB of HBM per device.

v0:
```python
import jax
import jax.numpy as jnp
from jax import lax
from jax.sharding import PartitionSpec as P

star_mass = 1.0


def entering(part, axis, combine, identity):
    place = lax.axis_index(axis)
    gathered = lax.all_gather(part, axis)
    state = jnp.zeros_like(part) + jnp.asarray(identity, part.dtype)

    def one(lap, state):
        return combine(state, lax.dynamic_index_in_dim(gathered, lap, 0, False))

    return lax.fori_loop(0, place, one, state)


def passed_along(value, axis, steps):
    count = lax.axis_size(axis)
    pairs = [(source, (source + steps) % count) for source in range(count)]
    return lax.ppermute(value, axis, pairs)


def with_halo(cells, sides, width, closed):
    for axis, dim in sides:
        count = lax.axis_size(axis)
        ends = count if closed else count - 1
        head = lax.slice_in_dim(cells, 0, width, axis=dim)
        tail = lax.slice_in_dim(cells, cells.shape[dim] - width, cells.shape[dim], axis=dim)
        cells = jnp.concatenate(
            [
                lax.ppermute(tail, axis, [(i, (i + 1) % count) for i in range(ends)]),
                cells,
                lax.ppermute(head, axis, [((i + 1) % count, i) for i in range(ends)]),
            ],
            axis=dim,
        )
    return cells


def add_totals(earlier, later):
    return earlier + later


def roll_by_bits(values, amounts, bit_total, axis):
    for bit_level in range(bit_total):
        rolled = jnp.roll(values, 1 << bit_level, axis=axis)
        chosen = amounts >> bit_level & 1 == 1
        values = jnp.where(chosen, rolled, values)
    return values


def cross_cells(current, previous, remain):
    cells_dev = current.shape[3]
    joined = jnp.concatenate([previous, current], axis=3)
    bit_total = max((cells_dev - 1).bit_length(), 1)
    moved = roll_by_bits(joined, remain[None, None, :, None], bit_total, 3)
    return moved[:, :, :, cells_dev:]


def shards(fields, shifts, cycle_area, gravity, kappa_az, kappa_rad):
    cells_dev = fields.shape[3]
    cycle_size = lax.axis_size("az")
    cycle_cells = cells_dev * cycle_size
    density = fields[0]
    local_mass = jnp.sum(density, axis=(0, 2))
    row_mass = cycle_area * lax.psum(local_mass, "az") / (2.0 * cycle_cells)
    before = jnp.cumsum(row_mass) - row_mass
    block_mass = jnp.sum(row_mass)
    offset = entering(block_mass, "rad", add_totals, jnp.float32(0.0))
    enclosed = star_mass + offset + before + 0.5 * row_mass
    pull_rate = (gravity * enclosed)[None, :, None]
    momentum = fields[1] - pull_rate * density
    energy = fields[3] - pull_rate * fields[1]
    current = jnp.stack([density, momentum, fields[2], energy, fields[4]])
    device_steps = shifts // cells_dev
    remain = shifts - device_steps * cells_dev
    bit_count = cycle_size.bit_length() - 1
    for bit_level in range(bit_count):
        rolled = passed_along(current, "az", 1 << bit_level)
        chosen = device_steps >> bit_level & 1 == 1
        current = jnp.where(chosen[None, None, :, None], rolled, current)
    previous = passed_along(current, "az", 1)
    advected = cross_cells(current, previous, remain)
    cycle_pad = with_halo(advected, (("az", 3),), 1, True)
    beside_all = cycle_pad[:, :, :, 2:] + cycle_pad[:, :, :, :-2] - 2.0 * advected
    radial_pad = with_halo(advected, (("rad", 2),), 1, False)
    across = radial_pad[:, :, 2:] + radial_pad[:, :, :-2] - 2.0 * advected
    updated = (
        advected
        + kappa_az[None, None, :, None] * beside_all
        + kappa_rad[None, None, :, None] * across
    )
    return (updated, enclosed)


def solution(mesh):
    placed = (P(None, None, "rad", "az"), P("rad"), P("rad"), P("rad"), P("rad"), P("rad"))
    return jax.shard_map(
        shards,
        mesh=mesh,
        in_specs=placed,
        out_specs=(P(None, None, "rad", "az"), P("rad")),
        check_vma=False,
    )
```

profile of v0, /device:TPU:4, one launch (start us, length us, event | category | flops | bytes accessed | tf_op | source)
XLA Modules:
  0.0 239.5 jit_solution(2277479553399708031)
XLA Ops:
  0.6 0.0 copy-start
  0.6 0.0 copy-start.1
  0.7 1.1 slice_reduce_fusion
  1.8 38.4 %psum.7 = f32[96]{0:T(128)S(1)} all-reduce(f32[96]{0:T(128)S(1)} %get-tuple-element.43), channel_id=1, replica_groups=mesh['az'=16,'rad'=2] {'az'}, use_global_device_ids=true, to_apply=%region_1.0 | all-reduce | flops 96 | bytes 768 | tf_op jit(solution)/shard_map/psum | solution.py:69
  40.2 1.2 dynamic-slice
  41.4 1.3 fusion.11
  42.7 1.3 dynamic-update-slice
  44.0 2.4 %all-reduce = f32[2]{0:T(128)S(1)} all-reduce(f32[2]{0:T(128)S(1)} %dynamic-update-slice), channel_id=1, replica_groups=mesh['az'=16,'rad'=2] {'rad'}, use_global_device_ids=true, to_apply=%add | all-reduce | flops 2 | bytes 16
  46.4 0.1 copy.9
  46.5 0.1 reduce-window.9
  46.7 0.1 reduce.1
  46.8 1.2 fusion.12
  48.0 1.1 subtract_dynamic-update-slice_fusion.1
  49.1 0.9 slice_dynamic-update-slice_fusion.1
  50.0 0.0 copy-done
  50.0 0.1 subtract_dynamic-update-slice_fusion
  50.2 0.1 collective-permute-start
  50.2 0.0 copy-done.1
  50.3 25.2 %collective-permute-done = f32[5,2,96,256]{3,2,1,0:T(8,128)S(1)} collective-permute-done((f32[5,2,96,256]{3,2,1,0:T(8,128)S(1)}, f32[5,2,96,256]{3,2,1,0:T(8,128)S(1)}, u32[]{:S(2)}, u32[]{:S(2)}) %collective-permute-start) | collective-permute-done | bytes 983072 | tf_op jit(solution)/shard_map/ppermute | solution.py:23
  75.5 0.2 broadcast_select_fusion
  75.7 0.1 collective-permute-start.1
  75.7 28.9 %collective-permute-done.1 = f32[5,2,96,256]{3,2,1,0:T(8,128)S(1)} collective-permute-done((f32[5,2,96,256]{3,2,1,0:T(8,128)S(1)}, f32[5,2,96,256]{3,2,1,0:T(8,128)S(1)}, u32[]{:S(2)}, u32[]{:S(2)}) %collective-permute-start.1) | collective-permute-done | bytes 983072 | tf_op jit(solution)/shard_map/ppermute | solution.py:23
  104.6 0.2 broadcast_select_fusion.1
  104.8 0.1 collective-permute-start.2
  104.8 25.0 %collective-permute-done.2 = f32[5,2,96,256]{3,2,1,0:T(8,128)S(1)} collective-permute-done((f32[5,2,96,256]{3,2,1,0:T(8,128)S(1)}, f32[5,2,96,256]{3,2,1,0:T(8,128)S(1)}, u32[]{:S(2)}, u32[]{:S(2)}) %collective-permute-start.2) | collective-permute-done | bytes 983072 | tf_op jit(solution)/shard_map/ppermute | solution.py:23
  129.9 0.2 broadcast_select_fusion.2
  130.1 0.1 collective-permute-start.3
  130.2 42.5 %collective-permute-done.3 = f32[5,2,96,256]{3,2,1,0:T(8,128)S(1)} collective-permute-done((f32[5,2,96,256]{3,2,1,0:T(8,128)S(1)}, f32[5,2,96,256]{3,2,1,0:T(8,128)S(1)}, u32[]{:S(2)}, u32[]{:S(2)}) %collective-permute-start.3) | collective-permute-done | bytes 983072 | tf_op jit(solution)/shard_map/ppermute | solution.py:23
  172.7 0.2 broadcast_select_fusion.3
  172.9 0.1 collective-permute-start.4
  173.0 0.2 slice.146
  173.2 24.4 %collective-permute-done.4 = f32[5,2,96,256]{3,2,1,0:T(8,128)S(1)} collective-permute-done((f32[5,2,96,256]{3,2,1,0:T(8,128)S(1)}, f32[5,2,96,256]{3,2,1,0:T(8,128)S(1)}, u32[]{:S(2)}, u32[]{:S(2)}) %collective-permute-start.4) | collective-permute-done | bytes 983072 | tf_op jit(solution)/shard_map/ppermute | solution.py:23
  197.5 0.3 fusion
  197.8 0.6 fusion.1
  198.4 0.2 slice.149
  198.6 0.6 maximum_select_fusion
  199.2 0.2 slice.151
  199.4 0.6 maximum_select_fusion.1
  200.0 0.2 slice.153
  200.2 0.6 maximum_select_fusion.2
  200.9 0.2 slice.155
  201.1 0.6 maximum_select_fusion.3
  201.7 0.2 slice.157
  201.9 0.6 maximum_select_fusion.4
  202.5 0.2 slice.159
  202.7 0.6 maximum_select_fusion.5
  203.4 0.1 slice.161
  203.5 0.1 slice.162
  203.6 0.4 maximum_select_fusion.6
  204.0 1.3 collective-permute-start.7
  205.3 0.0 copy-start.2
  205.3 0.0 copy-start.3
  205.3 3.0 %collective-permute-start.8 = (f32[5,2,1,256]{3,2,1,0:T(1,128)S(1)}, f32[5,2,1,256]{3,2,1,0:T(1,128)S(1)}, u32[]{:S(2)}, u32[]{:S(2)}) collective-permute-start(f32[5,2,1,256]{3,2,1,0:T(1,128)S(1)} %get-tuple-element.42), channel_id=1, source_target_pairs={{0,1},{2,3},{4,5},{6,7},{8,9},{10,11},{12,13},{14,15},{16,17},{18,... | collective-permute-start | bytes 30728 | tf_op jit(solution)/shard_map/ppermute | solution.py:34
  208.4 0.2 fusion.13
  208.6 2.6 %collective-permute-start.5 = (f32[5,2,96,1]{3,2,1,0:T(8,128)S(1)}, f32[5,2,96,1]{3,2,1,0:T(8,128)S(1)}, u32[]{:S(2)}, u32[]{:S(2)}) collective-permute-start(f32[5,2,96,1]{3,2,1,0:T(8,128)S(1)} %get-tuple-element.39), channel_id=1, source_target_pairs={{2,0},{4,2},{6,4},{8,6},{10,8},{12,10},{14,12},{16,14},{18,16},{20... | collective-permute-start | bytes 11528 | tf_op jit(solution)/shard_map/ppermute | solution.py:36
  211.2 0.0 collective-permute-start.6
  211.2 0.1 slice.163
  211.3 20.4 %collective-permute-done.5 = f32[5,2,96,1]{3,2,1,0:T(8,128)S(1)} collective-permute-done((f32[5,2,96,1]{3,2,1,0:T(8,128)S(1)}, f32[5,2,96,1]{3,2,1,0:T(8,128)S(1)}, u32[]{:S(2)}, u32[]{:S(2)}) %collective-permute-start.5) | collective-permute-done | bytes 3872 | tf_op jit(solution)/shard_map/ppermute | solution.py:36
  231.7 5.9 %collective-permute-done.6 = f32[5,2,96,1]{3,2,1,0:T(8,128)S(1)} collective-permute-done((f32[5,2,96,1]{3,2,1,0:T(8,128)S(1)}, f32[5,2,96,1]{3,2,1,0:T(8,128)S(1)}, u32[]{:S(2)}, u32[]{:S(2)}) %collective-permute-start.6) | collective-permute-done | bytes 3872 | tf_op jit(solution)/shard_map/ppermute | solution.py:34
  237.6 0.0 collective-permute-done.7
  237.6 0.0 collective-permute-done.8
  237.6 0.0 copy-done.2
  237.6 0.0 copy-done.3
  237.6 1.9 fusion.5
  (7 shorter events, 0.1 us)
Async XLA Ops:
  0.6 49.4 %copy-start = (f32[5,2,96,256]{3,2,1,0:T(8,128)S(1)}, f32[5,2,96,256]{3,2,1,0:T(8,128)}, u32[]{:S(2)}) copy-start(f32[5,2,96,256]{3,2,1,0:T(8,128)} %param.8) | copy-start | bytes 2949124
  0.6 49.6 %copy-start.1 = (s32[96]{0:T(128)S(1)}, s32[96]{0:T(128)}, u32[]{:S(2)}) copy-start(s32[96]{0:T(128)} %param.9) | copy-start | bytes 1156
  50.2 25.3 %collective-permute-start = (f32[5,2,96,256]{3,2,1,0:T(8,128)S(1)}, f32[5,2,96,256]{3,2,1,0:T(8,128)S(1)}, u32[]{:S(2)}, u32[]{:S(2)}) collective-permute-start(f32[5,2,96,256]{3,2,1,0:T(8,128)S(1)} %slice_dynamic-update-slice_fusion), channel_id=1, source_target_pairs={{0,2},{2,4},{4,6},{6,8},{8,10},{10,12},{12,14},{14,16},{16,18},{18... | collective-permute-start | bytes 2949128 | tf_op jit(solution)/shard_map/ppermute | solution.py:23
  75.7 28.9 %collective-permute-start.1 = (f32[5,2,96,256]{3,2,1,0:T(8,128)S(1)}, f32[5,2,96,256]{3,2,1,0:T(8,128)S(1)}, u32[]{:S(2)}, u32[]{:S(2)}) collective-permute-start(f32[5,2,96,256]{3,2,1,0:T(8,128)S(1)} %broadcast_select_fusion), channel_id=1, source_target_pairs={{0,4},{2,6},{4,8},{6,10},{8,12},{10,14},{12,16},{14,18},{16,20},{1... | collective-permute-start | bytes 2949128 | tf_op jit(solution)/shard_map/ppermute | solution.py:23
  104.8 25.1 %collective-permute-start.2 = (f32[5,2,96,256]{3,2,1,0:T(8,128)S(1)}, f32[5,2,96,256]{3,2,1,0:T(8,128)S(1)}, u32[]{:S(2)}, u32[]{:S(2)}) collective-permute-start(f32[5,2,96,256]{3,2,1,0:T(8,128)S(1)} %broadcast_select_fusion.1), channel_id=1, source_target_pairs={{0,8},{2,10},{4,12},{6,14},{8,16},{10,18},{12,20},{14,22},{16,24},... | collective-permute-start | bytes 2949128 | tf_op jit(solution)/shard_map/ppermute | solution.py:23
  130.1 42.6 %collective-permute-start.3 = (f32[5,2,96,256]{3,2,1,0:T(8,128)S(1)}, f32[5,2,96,256]{3,2,1,0:T(8,128)S(1)}, u32[]{:S(2)}, u32[]{:S(2)}) collective-permute-start(f32[5,2,96,256]{3,2,1,0:T(8,128)S(1)} %broadcast_select_fusion.2), channel_id=1, source_target_pairs={{0,16},{2,18},{4,20},{6,22},{8,24},{10,26},{12,28},{14,30},{16,0},... | collective-permute-start | bytes 2949128 | tf_op jit(solution)/shard_map/ppermute | solution.py:23
  172.9 24.6 %collective-permute-start.4 = (f32[5,2,96,256]{3,2,1,0:T(8,128)S(1)}, f32[5,2,96,256]{3,2,1,0:T(8,128)S(1)}, u32[]{:S(2)}, u32[]{:S(2)}) collective-permute-start(f32[5,2,96,256]{3,2,1,0:T(8,128)S(1)} %broadcast_select_fusion.3), channel_id=1, source_target_pairs={{0,2},{2,4},{4,6},{6,8},{8,10},{10,12},{12,14},{14,16},{16,18},{18... | collective-permute-start | bytes 2949128 | tf_op jit(solution)/shard_map/ppermute | solution.py:23
  204.0 33.5 %collective-permute-start.7 = (f32[5,2,1,256]{3,2,1,0:T(1,128)S(1)}, f32[5,2,1,256]{3,2,1,0:T(1,128)S(1)}, u32[]{:S(2)}, u32[]{:S(2)}) collective-permute-start(f32[5,2,1,256]{3,2,1,0:T(1,128)S(1)} %get-tuple-element.41), channel_id=1, source_target_pairs={{1,0},{3,2},{5,4},{7,6},{9,8},{11,10},{13,12},{15,14},{17,16},{19,... | collective-permute-start | bytes 30728 | tf_op jit(solution)/shard_map/ppermute | solution.py:36
  205.3 32.3 %copy-start.2 = (f32[96]{0:T(128)S(1)}, f32[96]{0:T(128)}, u32[]{:S(2)}) copy-start(f32[96]{0:T(128)} %param.13) | copy-start | bytes 1156
  205.3 32.2 %copy-start.3 = (f32[96]{0:T(128)S(1)}, f32[96]{0:T(128)}, u32[]{:S(2)}) copy-start(f32[96]{0:T(128)} %param.12) | copy-start | bytes 1156
  205.3 32.2 %collective-permute-start.8 = (f32[5,2,1,256]{3,2,1,0:T(1,128)S(1)}, f32[5,2,1,256]{3,2,1,0:T(1,128)S(1)}, u32[]{:S(2)}, u32[]{:S(2)}) collective-permute-start(f32[5,2,1,256]{3,2,1,0:T(1,128)S(1)} %get-tuple-element.42), channel_id=1, source_target_pairs={{0,1},{2,3},{4,5},{6,7},{8,9},{10,11},{12,13},{14,15},{16,17},{18,... | collective-permute-start | bytes 30728 | tf_op jit(solution)/shard_map/ppermute | solution.py:34
  208.6 23.1 %collective-permute-start.5 = (f32[5,2,96,1]{3,2,1,0:T(8,128)S(1)}, f32[5,2,96,1]{3,2,1,0:T(8,128)S(1)}, u32[]{:S(2)}, u32[]{:S(2)}) collective-permute-start(f32[5,2,96,1]{3,2,1,0:T(8,128)S(1)} %get-tuple-element.39), channel_id=1, source_target_pairs={{2,0},{4,2},{6,4},{8,6},{10,8},{12,10},{14,12},{16,14},{18,16},{20... | collective-permute-start | bytes 11528 | tf_op jit(solution)/shard_map/ppermute | solution.py:36
  211.2 26.4 %collective-permute-start.6 = (f32[5,2,96,1]{3,2,1,0:T(8,128)S(1)}, f32[5,2,96,1]{3,2,1,0:T(8,128)S(1)}, u32[]{:S(2)}, u32[]{:S(2)}) collective-permute-start(f32[5,2,96,1]{3,2,1,0:T(8,128)S(1)} %get-tuple-element.40), channel_id=1, source_target_pairs={{0,2},{2,4},{4,6},{6,8},{8,10},{10,12},{12,14},{14,16},{16,18},{18... | collective-permute-start | bytes 11528 | tf_op jit(solution)/shard_map/ppermute | solution.py:34
where the time goes:
time: 240 us; the launch traced here: 239 us
  waiting for transfers between devices  172 us (72%)
  blocking collectives  40.8 us (17%)
  other arithmetic  12.6 us (5%)
  starting transfers between devices  7.26 us (3%)
  local copies, waits for them, and re-layouts  5.5 us (2%)
    ppermute x5, waiting for transfers between devices, passed_along(): return lax.ppermute(value, axis, pairs)  146 us
    psum x1, blocking collectives, shards(): row_mass = cycle_area * lax.psum(local_mass, 'az') / (2.0 * cycle_cells)  38.4 us
    ppermute x2, waiting for transfers between devices, with_halo(): lax.ppermute(head, axis, [((i + 1) % count, i) for i in range(ends)])  20.4 us
    ppermute x2, waiting for transfers between devices, with_halo(): lax.ppermute(tail, axis, [(i, (i + 1) % count) for i in range(ends)])  5.89 us
  transfers between devices with their start and end apart: 9, of which 7 were waited for; matrix products, arithmetic and copies ran while one was open for 0% of the time, Pallas kernels for 0%

commit v1 on v0

v1 whole, which is shorter than its diff:
```python
import functools

import jax
import jax.numpy as jnp
from jax import lax
from jax.experimental import pallas as pl
from jax.experimental.pallas import tpu as pltpu
from jax.sharding import PartitionSpec as P

MESH = pl.DeviceIdType.MESH
SUB = 8
LANES = 128
star_mass = 1.0


def kernel(
    n, m, layers,
    fields, shifts, area, gravity, kappa_az, kappa_rad,
    out, enclosed_out,
    win, wout, adv, edge_out, edge_in, mass, total, shift_table, halo_in,
    send1, recv1, send2, recv2, mass_send, mass_recv, total_send, total_recv,
    edge_send, edge_recv, halo_send, halo_recv,
):
    slabs, rows, cols = fields.shape
    per_slab = rows // SUB
    groups = slabs * per_slab
    chunks = -(-groups // n)
    last = groups - n * (chunks - 1)
    me = lax.axis_index("az")
    ring = lax.axis_index("rad")

    def peer(step):
        return lax.rem(me + step, n)

    def rad_peer(step):
        return lax.rem(ring + step, m)

    def place(group):
        slab = lax.rem(group, slabs)
        block = lax.rem(per_slab - lax.div(group, slabs), per_slab)
        return slab, pl.ds(pl.multiple_of(block * SUB, SUB), SUB)

    def last_of(device):
        index = lax.div(device * last + n - 1, n)
        held = (index < last) & (lax.div(index * n, last) == device)
        return held, n * (chunks - 1) + index

    def to_peer(src, dst, send, recv, device):
        return pltpu.make_async_remote_copy(
            src_ref=src, dst_ref=dst, send_sem=send, recv_sem=recv,
            device_id={"az": device}, device_id_type=MESH,
        )

    def to_rad(src, dst, send, recv, device):
        return pltpu.make_async_remote_copy(
            src_ref=src, dst_ref=dst, send_sem=send, recv_sem=recv,
            device_id={"rad": device}, device_id_type=MESH,
        )

    def drain(ref, sem):
        pltpu.make_async_copy(ref, ref, sem).wait()

    def pieces(count):
        return win.at[0, pl.ds(0, count)]

    barrier = pltpu.get_barrier_semaphore()

    def greet(step, _):
        pl.semaphore_signal(barrier, inc=1, device_id={"az": peer(step)}, device_id_type=MESH)
        return 0

    def greet_rad(step, _):
        pl.semaphore_signal(barrier, inc=1, device_id={"rad": rad_peer(step)}, device_id_type=MESH)
        return 0

    lax.fori_loop(1, n, greet, 0)
    lax.fori_loop(1, m, greet_rad, 0)

    row_at = lax.broadcasted_iota(jnp.int32, (rows, LANES), 0)
    lane_at = lax.broadcasted_iota(jnp.int32, (rows, LANES), 1)
    square_row = lax.broadcasted_iota(jnp.int32, (rows, rows), 0)
    square_lane = lax.broadcasted_iota(jnp.int32, (rows, rows), 1)

    def as_column(line):
        return jnp.sum(jnp.where(square_row == square_lane, line, 0.0), axis=1, keepdims=True)

    density = fields[0]
    for z in range(1, layers):
        density = density + fields[z]
    local = jnp.sum(density, axis=1, keepdims=True)
    mass[me] = jnp.sum(jnp.where(row_at == lane_at, local, 0.0), axis=0, keepdims=True)

    pl.semaphore_wait(barrier, n - 1 + m - 1)

    def send_mass(step, _):
        to_peer(mass.at[me], mass.at[me], mass_send, mass_recv, peer(step)).start()
        return 0

    lax.fori_loop(1, n, send_mass, 0)

    def send_rows(chunk, _):
        def one(step, _):
            device = peer(step)
            slab, block = place(n * chunk + device)
            to_peer(
                fields.at[slab, block], win.at[chunk, me], send1.at[chunk], recv1.at[chunk], device
            ).start()
            return 0

        return lax.fori_loop(1, n, one, 0)

    lax.fori_loop(0, chunks - 1, send_rows, 0)

    def send_last(step, _):
        device = peer(step)
        held, group = last_of(device)

        @pl.when(held)
        def _():
            slab, block = place(group)
            to_peer(
                fields.at[slab, block], win.at[chunks - 1, me],
                send1.at[chunks - 1], recv1.at[chunks - 1], device,
            ).start()

        return 0

    lax.fori_loop(1, n, send_last, 0)

    drain(mass.at[pl.ds(0, n - 1)], mass_recv)
    cycle_mass = jnp.sum(mass[...], axis=0)[:, :rows]
    row_mass = area[...] * cycle_mass / (2.0 * (n * cols))
    block_mass = jnp.sum(row_mass, axis=1, keepdims=True)
    total[ring] = jnp.broadcast_to(block_mass, (1, LANES))

    def send_total(step, _):
        to_rad(total.at[ring], total.at[ring], total_send, total_recv, rad_peer(step)).start()
        return 0

    lax.fori_loop(1, m, send_total, 0)
    before = jnp.sum(jnp.where(square_lane < square_row, row_mass, 0.0), axis=1, keepdims=True)
    own = as_column(row_mass)
    drain(total.at[pl.ds(0, m - 1)], total_recv)
    rank = lax.broadcasted_iota(jnp.int32, (m, 1, LANES), 0)
    offset = jnp.sum(jnp.where(rank < ring, total[...], 0.0), axis=0)[:, :1]
    enclosed = star_mass + offset + before + 0.5 * own
    enclosed_out[...] = jnp.sum(jnp.where(square_row == square_lane, enclosed, 0.0), axis=0, keepdims=True)
    pull = as_column(gravity[...]) * enclosed

    shift_column = as_column(shifts[...].astype(jnp.float32)).astype(jnp.int32)
    shift_rows = jnp.broadcast_to(shift_column, (rows, LANES))
    shift_table[...] = shift_rows

    cells = n * cols
    small = lax.broadcasted_iota(jnp.int32, (SUB, LANES), 1)

    def roll_chunk(chunk, group):
        slab, block = place(group)
        win[chunk, me] = fields[slab, block, :]
        amount = shift_table[block, :]
        amount = amount[:, :1]
        row = jnp.concatenate([win[chunk, i] for i in range(n)], axis=1)
        for bit in range((cells - 1).bit_length()):
            rolled = pltpu.roll(row, 1 << bit, axis=1)
            row = jnp.where((amount >> bit) & 1 == 1, rolled, row)
        for i in range(n):
            wout[chunk, i] = row[:, i * cols:(i + 1) * cols]
        adv[slab, block, :] = wout[chunk, me]

        def back(step, _):
            device = peer(step)
            to_peer(
                wout.at[chunk, device], adv.at[slab, block], send2.at[chunk], recv2.at[chunk], device
            ).start()
            return 0

        lax.fori_loop(1, n, back, 0)
        for i in range(n):
            low = (i * cols - 1) % cells
            high = (i * cols + cols) % cells
            edge_out[i] = jnp.where(
                small == 2 * chunk, row[:, low:low + 1],
                jnp.where(small == 2 * chunk + 1, row[:, high:high + 1], edge_out[i]),
            )

    edge_out[...] = jnp.zeros(edge_out.shape, jnp.float32)

    def turn(chunk, _):
        drain(pieces(n - 1), recv1.at[chunk])
        roll_chunk(chunk, n * chunk + me)
        return 0

    lax.fori_loop(0, chunks - 1, turn, 0)
    held, group = last_of(me)

    @pl.when(held)
    def _():
        drain(pieces(n - 1), recv1.at[chunks - 1])
        roll_chunk(chunks - 1, group)

    edge_in[me] = edge_out[me]

    def send_edges(step, _):
        device = peer(step)
        to_peer(edge_out.at[device], edge_in.at[me], edge_send, edge_recv, device).start()
        return 0

    lax.fori_loop(1, n, send_edges, 0)

    def wait_back(chunk, _):
        drain(pieces(n - 1), recv2.at[chunk])
        return 0

    def wait_last(sem):
        @pl.when(held)
        def _():
            drain(pieces(last - 1), sem)

        @pl.when(jnp.logical_not(held))
        def _():
            drain(pieces(last), sem)

    early = min((2 * slabs - 1) // n + 1, chunks - 1)
    lax.fori_loop(0, early, wait_back, 0)

    for side, at in ((1, 0), (2, rows - 1)):
        rate = pull[at:at + 1, :]
        for slab in range(slabs):
            line = adv[slab, at:at + 1, :]
            if slab // layers in (1, 3):
                below = slab - layers if slab // layers == 1 else slab - 2 * layers
                line = line - rate * adv[below, at:at + 1, :]
            halo_in[side - 1, slab:slab + 1, :] = line
    to_rad(halo_in.at[0], halo_in.at[2], halo_send.at[0], halo_recv.at[0], rad_peer(m - 1)).start()
    to_rad(halo_in.at[1], halo_in.at[3], halo_send.at[1], halo_recv.at[1], rad_peer(1)).start()

    lax.fori_loop(early, chunks - 1, wait_back, 0)
    wait_last(recv2.at[chunks - 1])
    drain(edge_in.at[pl.ds(0, n - 1)], edge_recv)
    drain(halo_in.at[0], halo_recv.at[0])
    drain(halo_in.at[1], halo_recv.at[1])

    along = as_column(kappa_az[...])
    across = as_column(kappa_rad[...])
    wide_row = lax.broadcasted_iota(jnp.int32, (rows, cols), 0)
    wide_lane = lax.broadcasted_iota(jnp.int32, (rows, cols), 1)
    inner = ring > 0
    outer = ring < m - 1

    def ends(slab):
        sides = ([], [])
        for block in range(per_slab):
            index = ((per_slab - block) % per_slab) * slabs + slab
            chunk = index // n
            device = index % n if chunk < chunks - 1 else (index - n * chunk) * n // last
            for side in range(2):
                sides[side].append(edge_in[device, :, 2 * chunk + side:2 * chunk + side + 1])
        return jnp.concatenate(sides[0], axis=0), jnp.concatenate(sides[1], axis=0)

    for slab in range(slabs):
        here = adv[slab]
        left, right = ends(slab)
        if slab // layers in (1, 3):
            below = slab - layers if slab // layers == 1 else slab - 2 * layers
            here = here - pull * adv[below]
            other_left, other_right = ends(below)
            left = left - pull * other_left
            right = right - pull * other_right
        top = jnp.where(inner, halo_in[3, slab:slab + 1, :], 0.0)
        bottom = jnp.where(outer, halo_in[2, slab:slab + 1, :], 0.0)
        lower = jnp.where(wide_lane == 0, left, pltpu.roll(here, 1, axis=1))
        upper = jnp.where(wide_lane == cols - 1, right, pltpu.roll(here, cols - 1, axis=1))
        above = jnp.where(wide_row == 0, top, pltpu.roll(here, 1, axis=0))
        beneath = jnp.where(wide_row == rows - 1, bottom, pltpu.roll(here, rows - 1, axis=0))
        twice = 2.0 * here
        out[slab] = (
            here + along * (lower + upper - twice) + across * (beneath + above - twice)
        )

    drain(mass.at[pl.ds(0, n - 1)], mass_send)
    drain(total.at[pl.ds(0, m - 1)], total_send)
    drain(edge_in.at[pl.ds(0, n - 1)], edge_send)
    drain(halo_in.at[0], halo_send.at[0])
    drain(halo_in.at[1], halo_send.at[1])

    def wait_sent(chunk, _):
        drain(pieces(n - 1), send1.at[chunk])
        drain(pieces(n - 1), send2.at[chunk])
        return 0

    lax.fori_loop(0, chunks - 1, wait_sent, 0)
    wait_last(send1.at[chunks - 1])

    @pl.when(held)
    def _():
        drain(pieces(n - 1), send2.at[chunks - 1])


def shards(n, m, fields, shifts, area, gravity, kappa_az, kappa_rad):
    kinds, layers, rows, cols = fields.shape
    slabs = kinds * layers
    chunks = -(-(slabs * (rows // SUB)) // n)
    line = (1, rows)
    f32 = jnp.float32
    dma = pltpu.SemaphoreType.DMA
    vmem = pl.BlockSpec(memory_space=pltpu.VMEM)
    slab_pad = -(-slabs // SUB) * SUB
    updated, enclosed = pl.pallas_call(
        functools.partial(kernel, n, m, layers),
        out_shape=(
            jax.ShapeDtypeStruct((slabs, rows, cols), f32),
            jax.ShapeDtypeStruct(line, f32),
        ),
        in_specs=[vmem] * 6,
        out_specs=(vmem, vmem),
        scratch_shapes=[
            pltpu.VMEM((chunks, n, SUB, cols), f32),
            pltpu.VMEM((chunks, n, SUB, cols), f32),
            pltpu.VMEM((slabs, rows, cols), f32),
            pltpu.VMEM((n, SUB, LANES), f32),
            pltpu.VMEM((n, SUB, LANES), f32),
            pltpu.VMEM((n, 1, LANES), f32),
            pltpu.VMEM((m, 1, LANES), f32),
            pltpu.VMEM((rows, LANES), jnp.int32),
            pltpu.VMEM((4, slab_pad, cols), f32),
            dma((chunks,)), dma((chunks,)), dma((chunks,)), dma((chunks,)),
            dma, dma, dma, dma, dma, dma, dma((2,)), dma((2,)),
        ],
        compiler_params=pltpu.CompilerParams(
            collective_id=0, has_side_effects=True, vmem_limit_bytes=32 * 1024 * 1024
        ),
    )(
        fields.reshape(slabs, rows, cols), shifts.reshape(line), area.reshape(line),
        gravity.reshape(line), kappa_az.reshape(line), kappa_rad.reshape(line),
    )
    return updated.reshape(fields.shape), enclosed.reshape(rows)


def solution(mesh):
    placed = (P(None, None, "rad", "az"), P("rad"), P("rad"), P("rad"), P("rad"), P("rad"))
    return jax.shard_map(
        functools.partial(shards, mesh.shape["az"], mesh.shape["rad"]),
        mesh=mesh,
        in_specs=placed,
        out_specs=(P(None, None, "rad", "az"), P("rad")),
        check_vma=False,
    )
```

time: 240 us -> 59.3 us (0.25)
  the two profiles are of different devices: /device:TPU:4 before, /device:TPU:0 now
where the time goes in v1:
time: 59.3 us; the launch traced here: 59.1 us
  Pallas kernels  55.1 us (93%)
  local copies, waits for them, and re-layouts  3.34 us (6%)
  between operations  0.68 us (1%)
    pallas_call x1, Pallas kernels, shards(): pl.pallas_call(functools.partial(kernel, n, m, layers), out_shape=(jax.Sh...  55.1 us
    unnamed x14, local copies, waits for them, and re-layouts  3.34 us

profile of v1, /device:TPU:0, one launch (start us, length us, event | category | flops | bytes accessed | tf_op | source)
XLA Modules:
  0.0 59.1 jit_solution(15778210751529854964)
XLA Ops:
  0.6 0.0 copy-start.4
  0.6 0.0 copy-start.5
  0.7 0.0 copy-start.1
  0.7 0.0 copy-start.2
  0.7 0.0 copy-start.3
  0.7 0.6 %copy-done.4 = f32[96]{0:T(128)S(1)} copy-done((f32[96]{0:T(128)S(1)}, f32[96]{0:T(128)}, u32[]{:S(2)}) %copy-start.4) | copy-done | bytes 408
  1.3 0.0 copy-done.5
  1.3 0.0 copy-done.1
  1.3 0.0 copy-done.2
  1.3 0.0 copy-done.3
  1.4 0.0 copy-start
  1.4 1.2 %copy-done = f32[5,2,96,256]{3,2,1,0:T(8,128)S(1)} copy-done((f32[5,2,96,256]{3,2,1,0:T(8,128)S(1)}, f32[5,2,96,256]{3,2,1,0:T(8,128)}, u32[]{:S(2)}) %copy-start) | copy-done | bytes 983064
  2.6 55.1 %shard_map.77 = (f32[10,96,256]{2,1,0:T(8,128)S(1)}, f32[1,96]{1,0:T(1,128)S(1)}) custom-call(f32[10,96,256]{2,1,0:T(8,128)S(1)} %bitcast.8, s32[1,96]{1,0:T(1,128)S(1)} %bitcast.10, f32[1,96]{1,0:T(1,128)S(1)} %bitcast.11, f32[1,96]{1,0:T(1,128)S(1)} %bitcast.12, f32[1,96]{1,0:T(1,128)S(1)} %bitcast.13, f32[1,96]{1,0:T(1,128)S(1)} %bitcast.14), custom_call_target="tpu_custom_call" | custom-call | tf_op jit(solution)/shard_map/pallas_call | solution.py:308
  57.6 0.9 %copy.10 = f32[5,2,96,256]{3,2,1,0:T(8,128)} copy(f32[5,2,96,256]{3,2,1,0:T(8,128)S(1)} %bitcast.9) | data formatting | bytes 1966080
  58.6 0.5 copy.11
Async XLA Ops:
  0.6 0.7 %copy-start.4 = (f32[96]{0:T(128)S(1)}, f32[96]{0:T(128)}, u32[]{:S(2)}) copy-start(f32[96]{0:T(128)} %param.10) | copy-start | bytes 1156
  0.6 0.7 %copy-start.5 = (f32[96]{0:T(128)S(1)}, f32[96]{0:T(128)}, u32[]{:S(2)}) copy-start(f32[96]{0:T(128)} %param.11) | copy-start | bytes 1156
  0.7 0.7 %copy-start.1 = (s32[96]{0:T(128)S(1)}, s32[96]{0:T(128)}, u32[]{:S(2)}) copy-start(s32[96]{0:T(128)} %param.7) | copy-start | bytes 1156
  0.7 0.7 %copy-start.2 = (f32[96]{0:T(128)S(1)}, f32[96]{0:T(128)}, u32[]{:S(2)}) copy-start(f32[96]{0:T(128)} %param.8) | copy-start | bytes 1156
  0.7 0.7 %copy-start.3 = (f32[96]{0:T(128)S(1)}, f32[96]{0:T(128)}, u32[]{:S(2)}) copy-start(f32[96]{0:T(128)} %param.9) | copy-start | bytes 1156
  1.4 1.2 %copy-start = (f32[5,2,96,256]{3,2,1,0:T(8,128)S(1)}, f32[5,2,96,256]{3,2,1,0:T(8,128)}, u32[]{:S(2)}) copy-start(f32[5,2,96,256]{3,2,1,0:T(8,128)} %param.6) | copy-start | bytes 2949124

commit v2 on v1

--- a/solution.py
+++ b/solution.py
@@ -15,9 +15,10 @@
 
 def kernel(
     n, m, layers,
-    fields, shifts, area, gravity, kappa_az, kappa_rad,
+    source, shifts_in, area_in, gravity_in, kappa_az_in, kappa_rad_in,
     out, enclosed_out,
-    win, wout, adv, edge_out, edge_in, mass, total, shift_table, halo_in,
+    fields, shifts, area, gravity, kappa_az, kappa_rad, load_sem,
+    win, wout, adv, edge_sum, edge_out, edge_in, mass, total, shift_table, halo_in,
     send1, recv1, send2, recv2, mass_send, mass_recv, total_send, total_recv,
     edge_send, edge_recv, halo_send, halo_recv,
 ):
@@ -40,9 +41,14 @@
         block = lax.rem(per_slab - lax.div(group, slabs), per_slab)
         return slab, pl.ds(pl.multiple_of(block * SUB, SUB), SUB)
 
+    def owner(index):
+        if n == 2 * last:
+            return 2 * index + lax.rem(lax.div(index, 2) + index, 2)
+        return lax.div(index * n + n - 1, last)
+
     def last_of(device):
-        index = lax.div(device * last + n - 1, n)
-        held = (index < last) & (lax.div(index * n, last) == device)
+        index = lax.div(device * last, n)
+        held = owner(index) == device
         return held, n * (chunks - 1) + index
 
     def to_peer(src, dst, send, recv, device):
@@ -63,6 +69,16 @@
     def pieces(count):
         return win.at[0, pl.ds(0, count)]
 
+    loads = [
+        pltpu.make_async_copy(here, there, load_sem.at[i])
+        for i, (here, there) in enumerate((
+            (source, fields), (shifts_in, shifts), (area_in, area),
+            (gravity_in, gravity), (kappa_az_in, kappa_az), (kappa_rad_in, kappa_rad),
+        ))
+    ]
+    for load in loads:
+        load.start()
+
     barrier = pltpu.get_barrier_semaphore()
 
     def greet(step, _):
@@ -84,6 +100,8 @@
     def as_column(line):
         return jnp.sum(jnp.where(square_row == square_lane, line, 0.0), axis=1, keepdims=True)
 
+    for load in loads:
+        load.wait()
     density = fields[0]
     for z in range(1, layers):
         density = density + fields[z]
@@ -103,7 +121,7 @@
             device = peer(step)
             slab, block = place(n * chunk + device)
             to_peer(
-                fields.at[slab, block], win.at[chunk, me], send1.at[chunk], recv1.at[chunk], device
+                source.at[slab, block], win.at[chunk, me], send1.at[chunk], recv1.at[chunk], device
             ).start()
             return 0
 
@@ -119,40 +137,21 @@
         def _():
             slab, block = place(group)
             to_peer(
-                fields.at[slab, block], win.at[chunks - 1, me],
+                source.at[slab, block], win.at[chunks - 1, me],
                 send1.at[chunks - 1], recv1.at[chunks - 1], device,
             ).start()
 
         return 0
 
     lax.fori_loop(1, n, send_last, 0)
-
-    drain(mass.at[pl.ds(0, n - 1)], mass_recv)
-    cycle_mass = jnp.sum(mass[...], axis=0)[:, :rows]
-    row_mass = area[...] * cycle_mass / (2.0 * (n * cols))
-    block_mass = jnp.sum(row_mass, axis=1, keepdims=True)
-    total[ring] = jnp.broadcast_to(block_mass, (1, LANES))
-
-    def send_total(step, _):
-        to_rad(total.at[ring], total.at[ring], total_send, total_recv, rad_peer(step)).start()
-        return 0
-
-    lax.fori_loop(1, m, send_total, 0)
-    before = jnp.sum(jnp.where(square_lane < square_row, row_mass, 0.0), axis=1, keepdims=True)
-    own = as_column(row_mass)
-    drain(total.at[pl.ds(0, m - 1)], total_recv)
-    rank = lax.broadcasted_iota(jnp.int32, (m, 1, LANES), 0)
-    offset = jnp.sum(jnp.where(rank < ring, total[...], 0.0), axis=0)[:, :1]
-    enclosed = star_mass + offset + before + 0.5 * own
-    enclosed_out[...] = jnp.sum(jnp.where(square_row == square_lane, enclosed, 0.0), axis=0, keepdims=True)
-    pull = as_column(gravity[...]) * enclosed
 
     shift_column = as_column(shifts[...].astype(jnp.float32)).astype(jnp.int32)
     shift_rows = jnp.broadcast_to(shift_column, (rows, LANES))
     shift_table[...] = shift_rows
 
     cells = n * cols
-    small = lax.broadcasted_iota(jnp.int32, (SUB, LANES), 1)
+    spots = 2 * SUB
+    small = lax.broadcasted_iota(jnp.int32, (SUB, LANES), 1) - lax.broadcasted_iota(jnp.int32, (SUB, LANES), 0)
 
     def roll_chunk(chunk, group):
         slab, block = place(group)
@@ -178,12 +177,12 @@
         for i in range(n):
             low = (i * cols - 1) % cells
             high = (i * cols + cols) % cells
-            edge_out[i] = jnp.where(
-                small == 2 * chunk, row[:, low:low + 1],
-                jnp.where(small == 2 * chunk + 1, row[:, high:high + 1], edge_out[i]),
+            edge_sum[i] = jnp.where(
+                small == spots * chunk, row[:, low:low + 1],
+                jnp.where(small == spots * chunk + SUB, row[:, high:high + 1], edge_sum[i]),
             )
 
-    edge_out[...] = jnp.zeros(edge_out.shape, jnp.float32)
+    edge_sum[...] = jnp.zeros(edge_sum.shape, jnp.float32)
 
     def turn(chunk, _):
         drain(pieces(n - 1), recv1.at[chunk])
@@ -198,6 +197,7 @@
         drain(pieces(n - 1), recv1.at[chunks - 1])
         roll_chunk(chunks - 1, group)
 
+    edge_out[...] = jnp.sum(edge_sum[...], axis=1, keepdims=True)
     edge_in[me] = edge_out[me]
 
     def send_edges(step, _):
@@ -219,6 +219,26 @@
         @pl.when(jnp.logical_not(held))
         def _():
             drain(pieces(last), sem)
+
+    drain(mass.at[pl.ds(0, n - 1)], mass_recv)
+    cycle_mass = jnp.sum(mass[...], axis=0)[:, :rows]
+    row_mass = area[...] * cycle_mass / (2.0 * (n * cols))
+    block_mass = jnp.sum(row_mass, axis=1, keepdims=True)
+    total[ring] = jnp.broadcast_to(block_mass, (1, LANES))
+
+    def send_total(step, _):
+        to_rad(total.at[ring], total.at[ring], total_send, total_recv, rad_peer(step)).start()
+        return 0
+
+    lax.fori_loop(1, m, send_total, 0)
+    before = jnp.sum(jnp.where(square_lane < square_row, row_mass, 0.0), axis=1, keepdims=True)
+    own = as_column(row_mass)
+    drain(total.at[pl.ds(0, m - 1)], total_recv)
+    rank = lax.broadcasted_iota(jnp.int32, (m, 1, LANES), 0)
+    offset = jnp.sum(jnp.where(rank < ring, total[...], 0.0), axis=0)[:, :1]
+    enclosed = star_mass + offset + before + 0.5 * own
+    enclosed_out[...] = jnp.sum(jnp.where(square_row == square_lane, enclosed, 0.0), axis=0, keepdims=True)
+    pull = as_column(gravity[...]) * enclosed
 
     early = min((2 * slabs - 1) // n + 1, chunks - 1)
     lax.fori_loop(0, early, wait_back, 0)
@@ -247,23 +267,31 @@
     inner = ring > 0
     outer = ring < m - 1
 
+    def static_owner(index):
+        if n == 2 * last:
+            return 2 * index + (index // 2 + index) % 2
+        return (index * n + n - 1) // last
+
     def ends(slab):
         sides = ([], [])
         for block in range(per_slab):
             index = ((per_slab - block) % per_slab) * slabs + slab
             chunk = index // n
-            device = index % n if chunk < chunks - 1 else (index - n * chunk) * n // last
+            device = index % n if chunk < chunks - 1 else static_owner(index - n * chunk)
+            line = edge_in[device]
             for side in range(2):
-                sides[side].append(edge_in[device, :, 2 * chunk + side:2 * chunk + side + 1])
+                spot = jnp.where(small == spots * chunk + SUB * side, line, 0.0)
+                sides[side].append(jnp.sum(spot, axis=1, keepdims=True))
         return jnp.concatenate(sides[0], axis=0), jnp.concatenate(sides[1], axis=0)
 
+    edges = [ends(slab) for slab in range(slabs)]
     for slab in range(slabs):
         here = adv[slab]
-        left, right = ends(slab)
+        left, right = edges[slab]
         if slab // layers in (1, 3):
             below = slab - layers if slab // layers == 1 else slab - 2 * layers
             here = here - pull * adv[below]
-            other_left, other_right = ends(below)
+            other_left, other_right = edges[below]
             left = left - pull * other_left
             right = right - pull * other_right
         top = jnp.where(inner, halo_in[3, slab:slab + 1, :], 0.0)
@@ -304,6 +332,8 @@
     f32 = jnp.float32
     dma = pltpu.SemaphoreType.DMA
     vmem = pl.BlockSpec(memory_space=pltpu.VMEM)
+    hbm = pl.BlockSpec(memory_space=pltpu.HBM)
+    assert 2 * SUB * chunks <= LANES
     slab_pad = -(-slabs // SUB) * SUB
     updated, enclosed = pl.pallas_call(
         functools.partial(kernel, n, m, layers),
@@ -311,14 +341,19 @@
             jax.ShapeDtypeStruct((slabs, rows, cols), f32),
             jax.ShapeDtypeStruct(line, f32),
         ),
-        in_specs=[vmem] * 6,
+        in_specs=[hbm] * 6,
         out_specs=(vmem, vmem),
         scratch_shapes=[
+            pltpu.VMEM((slabs, rows, cols), f32),
+            pltpu.VMEM(line, jnp.int32),
+            pltpu.VMEM(line, f32), pltpu.VMEM(line, f32), pltpu.VMEM(line, f32), pltpu.VMEM(line, f32),
+            dma((6,)),
             pltpu.VMEM((chunks, n, SUB, cols), f32),
             pltpu.VMEM((chunks, n, SUB, cols), f32),
             pltpu.VMEM((slabs, rows, cols), f32),
             pltpu.VMEM((n, SUB, LANES), f32),
-            pltpu.VMEM((n, SUB, LANES), f32),
+            pltpu.VMEM((n, 1, LANES), f32),
+            pltpu.VMEM((n, 1, LANES), f32),
             pltpu.VMEM((n, 1, LANES), f32),
             pltpu.VMEM((m, 1, LANES), f32),
             pltpu.VMEM((rows, LANES), jnp.int32),

time: 59.3 us -> 56.7 us (0.956)
  Pallas kernels: 55.1 us -> 52.5 us
    pallas_call x1, Pallas kernels: 55.1 us -> 52.5 us  [shards(): pl.pallas_call(functools.partial(kernel, n, m, layers), out_shape=(jax.Sh...]
where the time goes in v2:
time: 56.7 us; the launch traced here: 56.5 us
  Pallas kernels  52.5 us (93%)
  local copies, waits for them, and re-layouts  3.34 us (6%)
  between operations  0.68 us (1%)
    pallas_call x1, Pallas kernels, shards(): pl.pallas_call(functools.partial(kernel, n, m, layers), out_shape=(jax.Sh...  52.5 us
    unnamed x14, local copies, waits for them, and re-layouts  3.34 us

profile of v2, /device:TPU:0, one launch (start us, length us, event | category | flops | bytes accessed | tf_op | source)
XLA Modules:
  0.0 56.5 jit_solution(10665839303663368282)
XLA Ops:
  0.6 0.0 copy-start.4
  0.6 0.0 copy-start.5
  0.7 0.0 copy-start.1
  0.7 0.0 copy-start.2
  0.7 0.0 copy-start.3
  0.7 0.6 %copy-done.4 = f32[96]{0:T(128)S(1)} copy-done((f32[96]{0:T(128)S(1)}, f32[96]{0:T(128)}, u32[]{:S(2)}) %copy-start.4) | copy-done | bytes 408
  1.3 0.0 copy-done.5
  1.3 0.0 copy-done.1
  1.3 0.0 copy-done.2
  1.3 0.0 copy-done.3
  1.4 0.0 copy-start
  1.4 1.2 %copy-done = f32[5,2,96,256]{3,2,1,0:T(8,128)S(1)} copy-done((f32[5,2,96,256]{3,2,1,0:T(8,128)S(1)}, f32[5,2,96,256]{3,2,1,0:T(8,128)}, u32[]{:S(2)}) %copy-start) | copy-done | bytes 983064
  2.6 52.5 %shard_map.77 = (f32[10,96,256]{2,1,0:T(8,128)S(1)}, f32[1,96]{1,0:T(1,128)S(1)}) custom-call(f32[10,96,256]{2,1,0:T(8,128)S(1)} %bitcast.8, s32[1,96]{1,0:T(1,128)S(1)} %bitcast.10, f32[1,96]{1,0:T(1,128)S(1)} %bitcast.11, f32[1,96]{1,0:T(1,128)S(1)} %bitcast.12, f32[1,96]{1,0:T(1,128)S(1)} %bitcast.13, f32[1,96]{1,0:T(1,128)S(1)} %bitcast.14), custom_call_target="tpu_custom_call" | custom-call | tf_op jit(solution)/shard_map/pallas_call | solution.py:338
  55.1 0.9 %copy.10 = f32[5,2,96,256]{3,2,1,0:T(8,128)} copy(f32[5,2,96,256]{3,2,1,0:T(8,128)S(1)} %bitcast.9) | data formatting | bytes 1966080
  56.0 0.5 copy.11
Async XLA Ops:
  0.6 0.7 %copy-start.4 = (f32[96]{0:T(128)S(1)}, f32[96]{0:T(128)}, u32[]{:S(2)}) copy-start(f32[96]{0:T(128)} %param.10) | copy-start | bytes 1156
  0.6 0.7 %copy-start.5 = (f32[96]{0:T(128)S(1)}, f32[96]{0:T(128)}, u32[]{:S(2)}) copy-start(f32[96]{0:T(128)} %param.11) | copy-start | bytes 1156
  0.7 0.7 %copy-start.1 = (s32[96]{0:T(128)S(1)}, s32[96]{0:T(128)}, u32[]{:S(2)}) copy-start(s32[96]{0:T(128)} %param.7) | copy-start | bytes 1156
  0.7 0.7 %copy-start.2 = (f32[96]{0:T(128)S(1)}, f32[96]{0:T(128)}, u32[]{:S(2)}) copy-start(f32[96]{0:T(128)} %param.8) | copy-start | bytes 1156
  0.7 0.7 %copy-start.3 = (f32[96]{0:T(128)S(1)}, f32[96]{0:T(128)}, u32[]{:S(2)}) copy-start(f32[96]{0:T(128)} %param.9) | copy-start | bytes 1156
  1.4 1.2 %copy-start = (f32[5,2,96,256]{3,2,1,0:T(8,128)S(1)}, f32[5,2,96,256]{3,2,1,0:T(8,128)}, u32[]{:S(2)}) copy-start(f32[5,2,96,256]{3,2,1,0:T(8,128)} %param.6) | copy-start | bytes 2949124

commit v3 on v2

--- a/solution.py
+++ b/solution.py
@@ -16,8 +16,8 @@
 def kernel(
     n, m, layers,
     source, shifts_in, area_in, gravity_in, kappa_az_in, kappa_rad_in,
-    out, enclosed_out,
-    fields, shifts, area, gravity, kappa_az, kappa_rad, load_sem,
+    out_hbm, enclosed_out,
+    out, out_sem, fields, shifts, area, gravity, kappa_az, kappa_rad, load_sem,
     win, wout, adv, edge_sum, edge_out, edge_in, mass, total, shift_table, halo_in,
     send1, recv1, send2, recv2, mass_send, mass_recv, total_send, total_recv,
     edge_send, edge_recv, halo_send, halo_recv,
@@ -33,6 +33,10 @@
     def peer(step):
         return lax.rem(me + step, n)
 
+    def far_peer(turn):
+        odd = lax.rem(turn, 2)
+        return peer(n // 2 + (lax.div(turn, 2) + odd) * (2 * odd - 1))
+
     def rad_peer(step):
         return lax.rem(ring + step, m)
 
@@ -117,20 +121,20 @@
     lax.fori_loop(1, n, send_mass, 0)
 
     def send_rows(chunk, _):
-        def one(step, _):
-            device = peer(step)
+        def one(turn, _):
+            device = far_peer(turn)
             slab, block = place(n * chunk + device)
             to_peer(
                 source.at[slab, block], win.at[chunk, me], send1.at[chunk], recv1.at[chunk], device
             ).start()
             return 0
 
-        return lax.fori_loop(1, n, one, 0)
+        return lax.fori_loop(0, n - 1, one, 0)
 
     lax.fori_loop(0, chunks - 1, send_rows, 0)
 
-    def send_last(step, _):
-        device = peer(step)
+    def send_last(turn, _):
+        device = far_peer(turn)
         held, group = last_of(device)
 
         @pl.when(held)
@@ -143,7 +147,7 @@
 
         return 0
 
-    lax.fori_loop(1, n, send_last, 0)
+    lax.fori_loop(0, n - 1, send_last, 0)
 
     shift_column = as_column(shifts[...].astype(jnp.float32)).astype(jnp.int32)
     shift_rows = jnp.broadcast_to(shift_column, (rows, LANES))
@@ -166,14 +170,14 @@
             wout[chunk, i] = row[:, i * cols:(i + 1) * cols]
         adv[slab, block, :] = wout[chunk, me]
 
-        def back(step, _):
-            device = peer(step)
+        def back(turn, _):
+            device = far_peer(turn)
             to_peer(
                 wout.at[chunk, device], adv.at[slab, block], send2.at[chunk], recv2.at[chunk], device
             ).start()
             return 0
 
-        lax.fori_loop(1, n, back, 0)
+        lax.fori_loop(0, n - 1, back, 0)
         for i in range(n):
             low = (i * cols - 1) % cells
             high = (i * cols + cols) % cells
@@ -304,7 +308,10 @@
         out[slab] = (
             here + along * (lower + upper - twice) + across * (beneath + above - twice)
         )
-
+        pltpu.make_async_copy(out.at[slab], out_hbm.at[slab], out_sem.at[slab]).start()
+
+    for slab in range(slabs):
+        pltpu.make_async_copy(out.at[slab], out_hbm.at[slab], out_sem.at[slab]).wait()
     drain(mass.at[pl.ds(0, n - 1)], mass_send)
     drain(total.at[pl.ds(0, m - 1)], total_send)
     drain(edge_in.at[pl.ds(0, n - 1)], edge_send)
@@ -342,8 +349,10 @@
             jax.ShapeDtypeStruct(line, f32),
         ),
         in_specs=[hbm] * 6,
-        out_specs=(vmem, vmem),
+        out_specs=(hbm, vmem),
         scratch_shapes=[
+            pltpu.VMEM((slabs, rows, cols), f32),
+            dma((slabs,)),
             pltpu.VMEM((slabs, rows, cols), f32),
             pltpu.VMEM(line, jnp.int32),
             pltpu.VMEM(line, f32), pltpu.VMEM(line, f32), pltpu.VMEM(line, f32), pltpu.VMEM(line, f32),
@@ -362,7 +371,7 @@
             dma, dma, dma, dma, dma, dma, dma((2,)), dma((2,)),
         ],
         compiler_params=pltpu.CompilerParams(
-            collective_id=0, has_side_effects=True, vmem_limit_bytes=32 * 1024 * 1024
+            collective_id=0, has_side_effects=True, vmem_limit_bytes=60 * 1024 * 1024
         ),
     )(
         fields.reshape(slabs, rows, cols), shifts.reshape(line), area.reshape(line),

time: 56.7 us -> 57.3 us (1.011)
  Pallas kernels: 52.5 us -> 53.7 us
  local copies, waits for them, and re-layouts: 3.34 us -> 2.73 us
    pallas_call x1, Pallas kernels: 52.5 us -> 53.7 us  [shards(): pl.pallas_call(functools.partial(kernel, n, m, layers), out_shape=(jax.Sh...]
    unnamed x14 -> x4, local copies, waits for them, and re-layouts: 3.34 us -> 2.73 us
where the time goes in v3:
time: 57.3 us; the launch traced here: 57.1 us
  Pallas kernels  53.7 us (94%)
  local copies, waits for them, and re-layouts  2.73 us (5%)
  between operations  0.65 us (1%)
    pallas_call x1, Pallas kernels, shards(): pl.pallas_call(functools.partial(kernel, n, m, layers), out_shape=(jax.Sh...  53.7 us
    unnamed x4, local copies, waits for them, and re-layouts  2.73 us

profile of v3, /device:TPU:0, one launch (start us, length us, event | category | flops | bytes accessed | tf_op | source)
XLA Modules:
  0.0 57.1 jit_solution(18279754339919207843)
XLA Ops:
  0.6 53.7 %shard_map.77 = (f32[10,96,256]{2,1,0:T(8,128)}, f32[1,96]{1,0:T(1,128)}) custom-call(f32[10,96,256]{2,1,0:T(8,128)} %bitcast.8, s32[1,96]{1,0:T(1,128)} %bitcast.10, f32[1,96]{1,0:T(1,128)} %bitcast.11, f32[1,96]{1,0:T(1,128)} %bitcast.12, f32[1,96]{1,0:T(1,128)} %bitcast.13, f32[1,96]{1,0:T(1,128)} %bitcast.14), custom_call_target="tpu_custom_call" | custom-call | tf_op jit(solution)/shard_map/pallas_call | solution.py:345
  54.4 0.0 copy-start
  54.4 2.2 %copy.10 = f32[5,2,96,256]{3,2,1,0:T(8,128)} copy(f32[5,2,96,256]{3,2,1,0:T(8,128)} %bitcast.9) | data formatting | bytes 1966080
  56.6 0.0 copy-done
  56.6 0.5 copy.11
Async XLA Ops:
  54.4 2.2 %copy-start = (f32[1,96]{1,0:T(1,128)S(1)}, f32[1,96]{1,0:T(1,128)}, u32[]{:S(2)}) copy-start(f32[1,96]{1,0:T(1,128)} %get-tuple-element.5) | copy-start | bytes 1156

commit v4 on v3

--- a/solution.py
+++ b/solution.py
@@ -9,6 +9,7 @@
 
 MESH = pl.DeviceIdType.MESH
 SUB = 8
+GROUP = 16
 LANES = 128
 star_mass = 1.0
 
@@ -23,7 +24,7 @@
     edge_send, edge_recv, halo_send, halo_recv,
 ):
     slabs, rows, cols = fields.shape
-    per_slab = rows // SUB
+    per_slab = rows // GROUP
     groups = slabs * per_slab
     chunks = -(-groups // n)
     last = groups - n * (chunks - 1)
@@ -43,16 +44,20 @@
     def place(group):
         slab = lax.rem(group, slabs)
         block = lax.rem(per_slab - lax.div(group, slabs), per_slab)
-        return slab, pl.ds(pl.multiple_of(block * SUB, SUB), SUB)
+        return slab, pl.ds(pl.multiple_of(block * GROUP, GROUP), GROUP)
 
     def owner(index):
-        if n == 2 * last:
-            return 2 * index + lax.rem(lax.div(index, 2) + index, 2)
-        return lax.div(index * n + n - 1, last)
+        if 4 * last == 3 * n:
+            return index // 3 * 4 + (index % 3 + 1 + index // 3) % 4
+        return (index * n + n - 1) // last
 
     def last_of(device):
+        if 4 * last == 3 * n:
+            four = lax.div(device, 4)
+            spot = lax.rem(device + 3 + 3 * four, 4)
+            return spot < 3, n * (chunks - 1) + 3 * four + spot
         index = lax.div(device * last, n)
-        held = owner(index) == device
+        held = lax.div(index * n + n - 1, last) == device
         return held, n * (chunks - 1) + index
 
     def to_peer(src, dst, send, recv, device):
@@ -154,20 +159,29 @@
     shift_table[...] = shift_rows
 
     cells = n * cols
-    spots = 2 * SUB
+    spots = 2 * GROUP
     small = lax.broadcasted_iota(jnp.int32, (SUB, LANES), 1) - lax.broadcasted_iota(jnp.int32, (SUB, LANES), 0)
 
     def roll_chunk(chunk, group):
         slab, block = place(group)
         win[chunk, me] = fields[slab, block, :]
-        amount = shift_table[block, :]
-        amount = amount[:, :1]
-        row = jnp.concatenate([win[chunk, i] for i in range(n)], axis=1)
-        for bit in range((cells - 1).bit_length()):
-            rolled = pltpu.roll(row, 1 << bit, axis=1)
-            row = jnp.where((amount >> bit) & 1 == 1, rolled, row)
-        for i in range(n):
-            wout[chunk, i] = row[:, i * cols:(i + 1) * cols]
+        amounts = shift_table[block, :]
+        for part in range(0, GROUP, SUB):
+            here = slice(part, part + SUB)
+            amount = amounts[here, :1]
+            row = jnp.concatenate([win[chunk, i, here] for i in range(n)], axis=1)
+            for bit in range((cells - 1).bit_length()):
+                rolled = pltpu.roll(row, 1 << bit, axis=1)
+                row = jnp.where((amount >> bit) & 1 == 1, rolled, row)
+            for i in range(n):
+                wout[chunk, i, here] = row[:, i * cols:(i + 1) * cols]
+                low = (i * cols - 1) % cells
+                high = (i * cols + cols) % cells
+                spot = spots * chunk + part
+                edge_sum[i] = jnp.where(
+                    small == spot, row[:, low:low + 1],
+                    jnp.where(small == spot + GROUP, row[:, high:high + 1], edge_sum[i]),
+                )
         adv[slab, block, :] = wout[chunk, me]
 
         def back(turn, _):
@@ -178,14 +192,6 @@
             return 0
 
         lax.fori_loop(0, n - 1, back, 0)
-        for i in range(n):
-            low = (i * cols - 1) % cells
-            high = (i * cols + cols) % cells
-            edge_sum[i] = jnp.where(
-                small == spots * chunk, row[:, low:low + 1],
-                jnp.where(small == spots * chunk + SUB, row[:, high:high + 1], edge_sum[i]),
-            )
-
     edge_sum[...] = jnp.zeros(edge_sum.shape, jnp.float32)
 
     def turn(chunk, _):
@@ -244,8 +250,10 @@
     enclosed_out[...] = jnp.sum(jnp.where(square_row == square_lane, enclosed, 0.0), axis=0, keepdims=True)
     pull = as_column(gravity[...]) * enclosed
 
-    early = min((2 * slabs - 1) // n + 1, chunks - 1)
-    lax.fori_loop(0, early, wait_back, 0)
+    early = (2 * slabs - 1) // n + 1
+    lax.fori_loop(0, min(early, chunks - 1), wait_back, 0)
+    if early == chunks:
+        wait_last(recv2.at[chunks - 1])
 
     for side, at in ((1, 0), (2, rows - 1)):
         rate = pull[at:at + 1, :]
@@ -258,8 +266,9 @@
     to_rad(halo_in.at[0], halo_in.at[2], halo_send.at[0], halo_recv.at[0], rad_peer(m - 1)).start()
     to_rad(halo_in.at[1], halo_in.at[3], halo_send.at[1], halo_recv.at[1], rad_peer(1)).start()
 
-    lax.fori_loop(early, chunks - 1, wait_back, 0)
-    wait_last(recv2.at[chunks - 1])
+    if early < chunks:
+        lax.fori_loop(early, chunks - 1, wait_back, 0)
+        wait_last(recv2.at[chunks - 1])
     drain(edge_in.at[pl.ds(0, n - 1)], edge_recv)
     drain(halo_in.at[0], halo_recv.at[0])
     drain(halo_in.at[1], halo_recv.at[1])
@@ -271,21 +280,17 @@
     inner = ring > 0
     outer = ring < m - 1
 
-    def static_owner(index):
-        if n == 2 * last:
-            return 2 * index + (index // 2 + index) % 2
-        return (index * n + n - 1) // last
-
     def ends(slab):
         sides = ([], [])
         for block in range(per_slab):
             index = ((per_slab - block) % per_slab) * slabs + slab
             chunk = index // n
-            device = index % n if chunk < chunks - 1 else static_owner(index - n * chunk)
+            device = index % n if chunk < chunks - 1 else owner(index - n * chunk)
             line = edge_in[device]
             for side in range(2):
-                spot = jnp.where(small == spots * chunk + SUB * side, line, 0.0)
-                sides[side].append(jnp.sum(spot, axis=1, keepdims=True))
+                for part in range(0, GROUP, SUB):
+                    spot = jnp.where(small == spots * chunk + GROUP * side + part, line, 0.0)
+                    sides[side].append(jnp.sum(spot, axis=1, keepdims=True))
         return jnp.concatenate(sides[0], axis=0), jnp.concatenate(sides[1], axis=0)
 
     edges = [ends(slab) for slab in range(slabs)]
@@ -334,13 +339,13 @@
 def shards(n, m, fields, shifts, area, gravity, kappa_az, kappa_rad):
     kinds, layers, rows, cols = fields.shape
     slabs = kinds * layers
-    chunks = -(-(slabs * (rows // SUB)) // n)
+    chunks = -(-(slabs * (rows // GROUP)) // n)
     line = (1, rows)
     f32 = jnp.float32
     dma = pltpu.SemaphoreType.DMA
     vmem = pl.BlockSpec(memory_space=pltpu.VMEM)
     hbm = pl.BlockSpec(memory_space=pltpu.HBM)
-    assert 2 * SUB * chunks <= LANES
+    assert 2 * GROUP * chunks <= LANES
     slab_pad = -(-slabs // SUB) * SUB
     updated, enclosed = pl.pallas_call(
         functools.partial(kernel, n, m, layers),
@@ -357,8 +362,8 @@
             pltpu.VMEM(line, jnp.int32),
             pltpu.VMEM(line, f32), pltpu.VMEM(line, f32), pltpu.VMEM(line, f32), pltpu.VMEM(line, f32),
             dma((6,)),
-            pltpu.VMEM((chunks, n, SUB, cols), f32),
-            pltpu.VMEM((chunks, n, SUB, cols), f32),
+            pltpu.VMEM((chunks, n, GROUP, cols), f32),
+            pltpu.VMEM((chunks, n, GROUP, cols), f32),
             pltpu.VMEM((slabs, rows, cols), f32),
             pltpu.VMEM((n, SUB, LANES), f32),
             pltpu.VMEM((n, 1, LANES), f32),

time: 57.3 us -> 58.3 us (1.017)
  Pallas kernels: 53.7 us -> 54.8 us
    pallas_call x1, Pallas kernels: 53.7 us -> 54.8 us  [shards(): pl.pallas_call(functools.partial(kernel, n, m, layers), out_shape=(jax.Sh...]
where the time goes in v4:
time: 58.3 us; the launch traced here: 58.2 us
  Pallas kernels  54.8 us (94%)
  local copies, waits for them, and re-layouts  2.73 us (5%)
  between operations  0.65 us (1%)
    pallas_call x1, Pallas kernels, shards(): pl.pallas_call(functools.partial(kernel, n, m, layers), out_shape=(jax.Sh...  54.8 us
    unnamed x4, local copies, waits for them, and re-layouts  2.73 us

profile of v4, /device:TPU:0, one launch (start us, length us, event | category | flops | bytes accessed | tf_op | source)
XLA Modules:
  0.0 58.2 jit_solution(12370855613507739923)
XLA Ops:
  0.6 54.8 %shard_map.77 = (f32[10,96,256]{2,1,0:T(8,128)}, f32[1,96]{1,0:T(1,128)}) custom-call(f32[10,96,256]{2,1,0:T(8,128)} %bitcast.8, s32[1,96]{1,0:T(1,128)} %bitcast.10, f32[1,96]{1,0:T(1,128)} %bitcast.11, f32[1,96]{1,0:T(1,128)} %bitcast.12, f32[1,96]{1,0:T(1,128)} %bitcast.13, f32[1,96]{1,0:T(1,128)} %bitcast.14), custom_call_target="tpu_custom_call" | custom-call | tf_op jit(solution)/shard_map/pallas_call | solution.py:350
  55.4 0.0 copy-start
  55.4 2.2 %copy.10 = f32[5,2,96,256]{3,2,1,0:T(8,128)} copy(f32[5,2,96,256]{3,2,1,0:T(8,128)} %bitcast.9) | data formatting | bytes 1966080
  57.7 0.0 copy-done
  57.7 0.5 copy.11
Async XLA Ops:
  55.4 2.2 %copy-start = (f32[1,96]{1,0:T(1,128)S(1)}, f32[1,96]{1,0:T(1,128)}, u32[]{:S(2)}) copy-start(f32[1,96]{1,0:T(1,128)} %get-tuple-element.5) | copy-start | bytes 1156

commit v5 on v4

--- a/solution.py
+++ b/solution.py
@@ -9,17 +9,28 @@
 
 MESH = pl.DeviceIdType.MESH
 SUB = 8
-GROUP = 16
+GROUP = 8
 LANES = 128
 star_mass = 1.0
 
 
-def kernel(
+def owner(n, last, index):
+    if n == 2 * last:
+        return 2 * index + (index // 2 + index) % 2
+    return (index * n + n - 1) // last
+
+
+def source_of(slab, layers):
+    return slab - {1: layers, 3: 2 * layers}.get(slab // layers, 0)
+
+
+def exchange(
     n, m, layers,
-    source, shifts_in, area_in, gravity_in, kappa_az_in, kappa_rad_in,
-    out_hbm, enclosed_out,
-    out, out_sem, fields, shifts, area, gravity, kappa_az, kappa_rad, load_sem,
-    win, wout, adv, edge_sum, edge_out, edge_in, mass, total, shift_table, halo_in,
+    source, shifts_in, area_in, gravity_in,
+    adv, edge_in, halo_in, enclosed_out,
+    fields, shifts, area, gravity, load_sem,
+    win, wout, edge_sum, edge_out, mass, total, shift_table, border, halo_out,
+    own_sem, border_sem,
     send1, recv1, send2, recv2, mass_send, mass_recv, total_send, total_recv,
     edge_send, edge_recv, halo_send, halo_recv,
 ):
@@ -46,19 +57,9 @@
         block = lax.rem(per_slab - lax.div(group, slabs), per_slab)
         return slab, pl.ds(pl.multiple_of(block * GROUP, GROUP), GROUP)
 
-    def owner(index):
-        if 4 * last == 3 * n:
-            return index // 3 * 4 + (index % 3 + 1 + index // 3) % 4
-        return (index * n + n - 1) // last
-
     def last_of(device):
-        if 4 * last == 3 * n:
-            four = lax.div(device, 4)
-            spot = lax.rem(device + 3 + 3 * four, 4)
-            return spot < 3, n * (chunks - 1) + 3 * four + spot
         index = lax.div(device * last, n)
-        held = lax.div(index * n + n - 1, last) == device
-        return held, n * (chunks - 1) + index
+        return owner(n, last, index) == device, n * (chunks - 1) + index
 
     def to_peer(src, dst, send, recv, device):
         return pltpu.make_async_remote_copy(
@@ -82,7 +83,7 @@
         pltpu.make_async_copy(here, there, load_sem.at[i])
         for i, (here, there) in enumerate((
             (source, fields), (shifts_in, shifts), (area_in, area),
-            (gravity_in, gravity), (kappa_az_in, kappa_az), (kappa_rad_in, kappa_rad),
+            (gravity_in, gravity),
         ))
     ]
     for load in loads:
@@ -182,7 +183,7 @@
                     small == spot, row[:, low:low + 1],
                     jnp.where(small == spot + GROUP, row[:, high:high + 1], edge_sum[i]),
                 )
-        adv[slab, block, :] = wout[chunk, me]
+        pltpu.make_async_copy(wout.at[chunk, me], adv.at[slab, block], own_sem.at[chunk]).start()
 
         def back(turn, _):
             device = far_peer(turn)
@@ -208,7 +209,8 @@
         roll_chunk(chunks - 1, group)
 
     edge_out[...] = jnp.sum(edge_sum[...], axis=1, keepdims=True)
-    edge_in[me] = edge_out[me]
+    own_edges = pltpu.make_async_copy(edge_out.at[me], edge_in.at[me], border_sem.at[2])
+    own_edges.start()
 
     def send_edges(step, _):
         device = peer(step)
@@ -219,12 +221,15 @@
 
     def wait_back(chunk, _):
         drain(pieces(n - 1), recv2.at[chunk])
-        return 0
-
-    def wait_last(sem):
+        drain(wout.at[0, 0], own_sem.at[chunk])
+        return 0
+
+    def wait_last(sem, own):
         @pl.when(held)
         def _():
             drain(pieces(last - 1), sem)
+            if own:
+                drain(wout.at[0, 0], own_sem.at[chunks - 1])
 
         @pl.when(jnp.logical_not(held))
         def _():
@@ -253,26 +258,91 @@
     early = (2 * slabs - 1) // n + 1
     lax.fori_loop(0, min(early, chunks - 1), wait_back, 0)
     if early == chunks:
-        wait_last(recv2.at[chunks - 1])
-
-    for side, at in ((1, 0), (2, rows - 1)):
+        wait_last(recv2.at[chunks - 1], True)
+
+    rims = [
+        pltpu.make_async_copy(adv.at[:, pl.ds(at, SUB)], border.at[side], border_sem.at[side])
+        for side, at in enumerate((0, rows - SUB))
+    ]
+    for rim in rims:
+        rim.start()
+    for rim in rims:
+        rim.wait()
+    for side, at, row in ((0, 0, 0), (1, rows - 1, SUB - 1)):
         rate = pull[at:at + 1, :]
         for slab in range(slabs):
-            line = adv[slab, at:at + 1, :]
-            if slab // layers in (1, 3):
-                below = slab - layers if slab // layers == 1 else slab - 2 * layers
-                line = line - rate * adv[below, at:at + 1, :]
-            halo_in[side - 1, slab:slab + 1, :] = line
-    to_rad(halo_in.at[0], halo_in.at[2], halo_send.at[0], halo_recv.at[0], rad_peer(m - 1)).start()
-    to_rad(halo_in.at[1], halo_in.at[3], halo_send.at[1], halo_recv.at[1], rad_peer(1)).start()
+            line = border[side, slab, row:row + 1, :]
+            below = source_of(slab, layers)
+            if below != slab:
+                line = line - rate * border[side, below, row:row + 1, :]
+            halo_out[side, slab:slab + 1, :] = line
+    to_rad(halo_out.at[0], halo_in.at[1], halo_send.at[0], halo_recv.at[0], rad_peer(m - 1)).start()
+    to_rad(halo_out.at[1], halo_in.at[0], halo_send.at[1], halo_recv.at[1], rad_peer(1)).start()
 
     if early < chunks:
         lax.fori_loop(early, chunks - 1, wait_back, 0)
-        wait_last(recv2.at[chunks - 1])
-    drain(edge_in.at[pl.ds(0, n - 1)], edge_recv)
-    drain(halo_in.at[0], halo_recv.at[0])
-    drain(halo_in.at[1], halo_recv.at[1])
-
+        wait_last(recv2.at[chunks - 1], True)
+    drain(edge_out.at[pl.ds(0, n - 1)], edge_recv)
+    drain(halo_out.at[0], halo_recv.at[0])
+    drain(halo_out.at[1], halo_recv.at[1])
+    own_edges.wait()
+
+    drain(mass.at[pl.ds(0, n - 1)], mass_send)
+    drain(total.at[pl.ds(0, m - 1)], total_send)
+    drain(edge_out.at[pl.ds(0, n - 1)], edge_send)
+    drain(halo_out.at[0], halo_send.at[0])
+    drain(halo_out.at[1], halo_send.at[1])
+
+    def wait_sent(chunk, _):
+        drain(pieces(n - 1), send1.at[chunk])
+        drain(pieces(n - 1), send2.at[chunk])
+        return 0
+
+    lax.fori_loop(0, chunks - 1, wait_sent, 0)
+    wait_last(send1.at[chunks - 1], False)
+
+    @pl.when(held)
+    def _():
+        drain(pieces(n - 1), send2.at[chunks - 1])
+
+def diffuse(
+    n, m, layers,
+    adv_in, edge_in, halo_in, enclosed_in, gravity_in, kappa_az_in, kappa_rad_in,
+    out_hbm, enclosed_out,
+    adv, edge_lines, halo, enclosed, gravity, kappa_az, kappa_rad, out, adv_sem, load_sem, out_sem,
+):
+    slabs, rows, cols = adv.shape
+    per_slab = rows // GROUP
+    groups = slabs * per_slab
+    chunks = -(-groups // n)
+    last = groups - n * (chunks - 1)
+    ring = lax.axis_index("rad")
+
+    loads = [
+        pltpu.make_async_copy(here, there, load_sem.at[i])
+        for i, (here, there) in enumerate((
+            (edge_in, edge_lines), (halo_in, halo), (enclosed_in, enclosed),
+            (gravity_in, gravity), (kappa_az_in, kappa_az), (kappa_rad_in, kappa_rad),
+        ))
+    ]
+    slab_loads = [
+        pltpu.make_async_copy(adv_in.at[slab], adv.at[slab], adv_sem.at[slab]) for slab in range(slabs)
+    ]
+    for load in loads + slab_loads:
+        load.start()
+
+    square_row = lax.broadcasted_iota(jnp.int32, (rows, rows), 0)
+    square_lane = lax.broadcasted_iota(jnp.int32, (rows, rows), 1)
+
+    def as_column(line):
+        return jnp.sum(jnp.where(square_row == square_lane, line, 0.0), axis=1, keepdims=True)
+
+    spots = 2 * GROUP
+    small = lax.broadcasted_iota(jnp.int32, (SUB, LANES), 1) - lax.broadcasted_iota(jnp.int32, (SUB, LANES), 0)
+    for load in loads:
+        load.wait()
+    enclosed_out[...] = enclosed[...]
+    pull = as_column(gravity[...]) * as_column(enclosed[...])
     along = as_column(kappa_az[...])
     across = as_column(kappa_rad[...])
     wide_row = lax.broadcasted_iota(jnp.int32, (rows, cols), 0)
@@ -285,8 +355,8 @@
         for block in range(per_slab):
             index = ((per_slab - block) % per_slab) * slabs + slab
             chunk = index // n
-            device = index % n if chunk < chunks - 1 else owner(index - n * chunk)
-            line = edge_in[device]
+            device = index % n if chunk < chunks - 1 else owner(n, last, index - n * chunk)
+            line = edge_lines[device]
             for side in range(2):
                 for part in range(0, GROUP, SUB):
                     spot = jnp.where(small == spots * chunk + GROUP * side + part, line, 0.0)
@@ -295,16 +365,17 @@
 
     edges = [ends(slab) for slab in range(slabs)]
     for slab in range(slabs):
+        slab_loads[slab].wait()
         here = adv[slab]
         left, right = edges[slab]
-        if slab // layers in (1, 3):
-            below = slab - layers if slab // layers == 1 else slab - 2 * layers
+        below = source_of(slab, layers)
+        if below != slab:
             here = here - pull * adv[below]
             other_left, other_right = edges[below]
             left = left - pull * other_left
             right = right - pull * other_right
-        top = jnp.where(inner, halo_in[3, slab:slab + 1, :], 0.0)
-        bottom = jnp.where(outer, halo_in[2, slab:slab + 1, :], 0.0)
+        top = jnp.where(inner, halo[0, slab:slab + 1, :], 0.0)
+        bottom = jnp.where(outer, halo[1, slab:slab + 1, :], 0.0)
         lower = jnp.where(wide_lane == 0, left, pltpu.roll(here, 1, axis=1))
         upper = jnp.where(wide_lane == cols - 1, right, pltpu.roll(here, cols - 1, axis=1))
         above = jnp.where(wide_row == 0, top, pltpu.roll(here, 1, axis=0))
@@ -317,23 +388,6 @@
 
     for slab in range(slabs):
         pltpu.make_async_copy(out.at[slab], out_hbm.at[slab], out_sem.at[slab]).wait()
-    drain(mass.at[pl.ds(0, n - 1)], mass_send)
-    drain(total.at[pl.ds(0, m - 1)], total_send)
-    drain(edge_in.at[pl.ds(0, n - 1)], edge_send)
-    drain(halo_in.at[0], halo_send.at[0])
-    drain(halo_in.at[1], halo_send.at[1])
-
-    def wait_sent(chunk, _):
-        drain(pieces(n - 1), send1.at[chunk])
-        drain(pieces(n - 1), send2.at[chunk])
-        return 0
-
-    lax.fori_loop(0, chunks - 1, wait_sent, 0)
-    wait_last(send1.at[chunks - 1])
-
-    @pl.when(held)
-    def _():
-        drain(pieces(n - 1), send2.at[chunks - 1])
 
 
 def shards(n, m, fields, shifts, area, gravity, kappa_az, kappa_rad):
@@ -347,41 +401,58 @@
     hbm = pl.BlockSpec(memory_space=pltpu.HBM)
     assert 2 * GROUP * chunks <= LANES
     slab_pad = -(-slabs // SUB) * SUB
-    updated, enclosed = pl.pallas_call(
-        functools.partial(kernel, n, m, layers),
+    whole = jax.ShapeDtypeStruct((slabs, rows, cols), f32)
+    params = pltpu.CompilerParams(vmem_limit_bytes=60 * 1024 * 1024)
+    one = jax.ShapeDtypeStruct(line, f32)
+    shifts, area, gravity, kappa_az, kappa_rad = (
+        value.reshape(line) for value in (shifts, area, gravity, kappa_az, kappa_rad)
+    )
+    adv, edges, halo, enclosed = pl.pallas_call(
+        functools.partial(exchange, n, m, layers),
         out_shape=(
-            jax.ShapeDtypeStruct((slabs, rows, cols), f32),
-            jax.ShapeDtypeStruct(line, f32),
+            whole,
+            jax.ShapeDtypeStruct((n, 1, LANES), f32),
+            jax.ShapeDtypeStruct((2, slab_pad, cols), f32),
+            one,
         ),
-        in_specs=[hbm] * 6,
-        out_specs=(hbm, vmem),
+        in_specs=[hbm] * 4,
+        out_specs=(hbm, hbm, hbm, vmem),
         scratch_shapes=[
             pltpu.VMEM((slabs, rows, cols), f32),
-            dma((slabs,)),
-            pltpu.VMEM((slabs, rows, cols), f32),
-            pltpu.VMEM(line, jnp.int32),
-            pltpu.VMEM(line, f32), pltpu.VMEM(line, f32), pltpu.VMEM(line, f32), pltpu.VMEM(line, f32),
-            dma((6,)),
+            pltpu.VMEM(line, jnp.int32), pltpu.VMEM(line, f32), pltpu.VMEM(line, f32),
+            dma((4,)),
             pltpu.VMEM((chunks, n, GROUP, cols), f32),
             pltpu.VMEM((chunks, n, GROUP, cols), f32),
-            pltpu.VMEM((slabs, rows, cols), f32),
             pltpu.VMEM((n, SUB, LANES), f32),
-            pltpu.VMEM((n, 1, LANES), f32),
             pltpu.VMEM((n, 1, LANES), f32),
             pltpu.VMEM((n, 1, LANES), f32),
             pltpu.VMEM((m, 1, LANES), f32),
             pltpu.VMEM((rows, LANES), jnp.int32),
-            pltpu.VMEM((4, slab_pad, cols), f32),
+            pltpu.VMEM((2, slabs, SUB, cols), f32),
+            pltpu.VMEM((2, slab_pad, cols), f32),
+            dma((chunks,)), dma((3,)),
             dma((chunks,)), dma((chunks,)), dma((chunks,)), dma((chunks,)),
             dma, dma, dma, dma, dma, dma, dma((2,)), dma((2,)),
         ],
         compiler_params=pltpu.CompilerParams(
             collective_id=0, has_side_effects=True, vmem_limit_bytes=60 * 1024 * 1024
         ),
-    )(
-        fields.reshape(slabs, rows, cols), shifts.reshape(line), area.reshape(line),
-        gravity.reshape(line), kappa_az.reshape(line), kappa_rad.reshape(line),
-    )
+    )(fields.reshape(slabs, rows, cols), shifts, area, gravity)
+    updated, enclosed = pl.pallas_call(
+        functools.partial(diffuse, n, m, layers),
+        out_shape=(whole, one),
+        in_specs=[hbm] * 7,
+        out_specs=(hbm, vmem),
+        scratch_shapes=[
+            pltpu.VMEM((slabs, rows, cols), f32),
+            pltpu.VMEM((n, 1, LANES), f32),
+            pltpu.VMEM((2, slab_pad, cols), f32),
+            pltpu.VMEM(line, f32), pltpu.VMEM(line, f32), pltpu.VMEM(line, f32), pltpu.VMEM(line, f32),
+            pltpu.VMEM((slabs, rows, cols), f32),
+            dma((slabs,)), dma((6,)), dma((slabs,)),
+        ],
+        compiler_params=params,
+    )(adv, edges, halo, enclosed, gravity, kappa_az, kappa_rad)
     return updated.reshape(fields.shape), enclosed.reshape(rows)
 
 

time: 58.3 us -> 57.1 us (0.979)
  local copies, waits for them, and re-layouts: 2.73 us -> 0 us
  Pallas kernels: 54.8 us -> 56.3 us
    unnamed x4 -> x0, local copies, waits for them, and re-layouts: 2.73 us -> none
    pallas_call x1 -> x2, Pallas kernels: 54.8 us -> 56.3 us  [the longest x1 51.9 us: shards(): pl.pallas_call(functools.partial(exchange, n, m, layers), out_shape=(whol...]
where the time goes in v5:
time: 57.1 us; the launch traced here: 56.9 us
  Pallas kernels  56.3 us (99%)
  between operations  0.64 us (1%)
    pallas_call x1, Pallas kernels, shards(): pl.pallas_call(functools.partial(exchange, n, m, layers), out_shape=(whol...  51.9 us
    pallas_call x1, Pallas kernels, shards(): pl.pallas_call(functools.partial(diffuse, n, m, layers), out_shape=(whole...  4.36 us

profile of v5, /device:TPU:0, one launch (start us, length us, event | category | flops | bytes accessed | tf_op | source)
XLA Modules:
  0.0 56.9 jit_solution(16262587220170936700)
XLA Ops:
  0.6 51.9 %shard_map.77 = (f32[10,96,256]{2,1,0:T(8,128)}, f32[16,1,128]{2,1,0:T(1,128)}, f32[2,16,256]{2,1,0:T(8,128)}, f32[1,96]{1,0:T(1,128)}) custom-call(f32[10,96,256]{2,1,0:T(8,128)} %bitcast.8, s32[1,96]{1,0:T(1,128)} %bitcast.11, f32[1,96]{1,0:T(1,128)} %bitcast.12, f32[1,96]{1,0:T(1,128)} %bitcast.9), custom_call_target="tpu_custom_call" | custom-call | tf_op jit(solution)/shard_map/pallas_call | solution.py:410
  52.6 4.4 %shard_map.78 = (f32[10,96,256]{2,1,0:T(8,128)}, f32[1,96]{1,0:T(1,128)}) custom-call(f32[10,96,256]{2,1,0:T(8,128)} %get-tuple-element.8.adv_in, f32[16,1,128]{2,1,0:T(1,128)} %get-tuple-element.9.edge_in, f32[2,16,256]{2,1,0:T(8,128)} %get-tuple-element.10.halo_in, f32[1,96]{1,0:T(1,128)} %get-tuple-element.11.enclosed_in, f32[1,96]{1,0:T(1,128)} %bitcast.10, ...), custom_call_target="tpu_custom_call" | custom-call | tf_op jit(solution)/shard_map/pallas_call | solution.py:441

commit v6 on v2

--- a/solution.py
+++ b/solution.py
@@ -18,7 +18,7 @@
     source, shifts_in, area_in, gravity_in, kappa_az_in, kappa_rad_in,
     out, enclosed_out,
     fields, shifts, area, gravity, kappa_az, kappa_rad, load_sem,
-    win, wout, adv, edge_sum, edge_out, edge_in, mass, total, shift_table, halo_in,
+    win, wout, adv, edge_out, edge_in, mass, total, shift_table, tables, halo_in,
     send1, recv1, send2, recv2, mass_send, mass_recv, total_send, total_recv,
     edge_send, edge_recv, halo_send, halo_recv,
 ):
@@ -150,7 +150,6 @@
     shift_table[...] = shift_rows
 
     cells = n * cols
-    spots = 2 * SUB
     small = lax.broadcasted_iota(jnp.int32, (SUB, LANES), 1) - lax.broadcasted_iota(jnp.int32, (SUB, LANES), 0)
 
     def roll_chunk(chunk, group):
@@ -177,12 +176,22 @@
         for i in range(n):
             low = (i * cols - 1) % cells
             high = (i * cols + cols) % cells
-            edge_sum[i] = jnp.where(
-                small == spots * chunk, row[:, low:low + 1],
-                jnp.where(small == spots * chunk + SUB, row[:, high:high + 1], edge_sum[i]),
+            ends = jnp.where(
+                small == 0, row[:, low:low + 1],
+                jnp.where(small == SUB, row[:, high:high + 1], 0.0),
             )
-
-    edge_sum[...] = jnp.zeros(edge_sum.shape, jnp.float32)
+            edge_out[chunk, i] = jnp.sum(ends, axis=0, keepdims=True)
+        edge_in[chunk, me] = edge_out[chunk, me]
+
+        def back_edges(step, _):
+            device = peer(step)
+            to_peer(
+                edge_out.at[chunk, device], edge_in.at[chunk, me],
+                edge_send.at[chunk], edge_recv.at[chunk], device,
+            ).start()
+            return 0
+
+        lax.fori_loop(1, n, back_edges, 0)
 
     def turn(chunk, _):
         drain(pieces(n - 1), recv1.at[chunk])
@@ -197,28 +206,17 @@
         drain(pieces(n - 1), recv1.at[chunks - 1])
         roll_chunk(chunks - 1, group)
 
-    edge_out[...] = jnp.sum(edge_sum[...], axis=1, keepdims=True)
-    edge_in[me] = edge_out[me]
-
-    def send_edges(step, _):
-        device = peer(step)
-        to_peer(edge_out.at[device], edge_in.at[me], edge_send, edge_recv, device).start()
-        return 0
-
-    lax.fori_loop(1, n, send_edges, 0)
-
-    def wait_back(chunk, _):
-        drain(pieces(n - 1), recv2.at[chunk])
-        return 0
-
-    def wait_last(sem):
+    def lines(count):
+        return edge_in.at[0, pl.ds(0, count)]
+
+    def wait_last(some, sem):
         @pl.when(held)
         def _():
-            drain(pieces(last - 1), sem)
+            drain(some(last - 1), sem)
 
         @pl.when(jnp.logical_not(held))
         def _():
-            drain(pieces(last), sem)
+            drain(some(last), sem)
 
     drain(mass.at[pl.ds(0, n - 1)], mass_recv)
     cycle_mass = jnp.sum(mass[...], axis=0)[:, :rows]
@@ -240,88 +238,120 @@
     enclosed_out[...] = jnp.sum(jnp.where(square_row == square_lane, enclosed, 0.0), axis=0, keepdims=True)
     pull = as_column(gravity[...]) * enclosed
 
-    early = min((2 * slabs - 1) // n + 1, chunks - 1)
-    lax.fori_loop(0, early, wait_back, 0)
-
-    for side, at in ((1, 0), (2, rows - 1)):
-        rate = pull[at:at + 1, :]
-        for slab in range(slabs):
-            line = adv[slab, at:at + 1, :]
-            if slab // layers in (1, 3):
-                below = slab - layers if slab // layers == 1 else slab - 2 * layers
-                line = line - rate * adv[below, at:at + 1, :]
-            halo_in[side - 1, slab:slab + 1, :] = line
-    to_rad(halo_in.at[0], halo_in.at[2], halo_send.at[0], halo_recv.at[0], rad_peer(m - 1)).start()
-    to_rad(halo_in.at[1], halo_in.at[3], halo_send.at[1], halo_recv.at[1], rad_peer(1)).start()
-
-    lax.fori_loop(early, chunks - 1, wait_back, 0)
-    wait_last(recv2.at[chunks - 1])
-    drain(edge_in.at[pl.ds(0, n - 1)], edge_recv)
-    drain(halo_in.at[0], halo_recv.at[0])
-    drain(halo_in.at[1], halo_recv.at[1])
-
-    along = as_column(kappa_az[...])
-    across = as_column(kappa_rad[...])
-    wide_row = lax.broadcasted_iota(jnp.int32, (rows, cols), 0)
-    wide_lane = lax.broadcasted_iota(jnp.int32, (rows, cols), 1)
-    inner = ring > 0
-    outer = ring < m - 1
+    tables[0] = jnp.broadcast_to(pull, (rows, LANES))
+    tables[1] = jnp.broadcast_to(as_column(kappa_az[...]), (rows, LANES))
+    tables[2] = jnp.broadcast_to(as_column(kappa_rad[...]), (rows, LANES))
+
+    def wide(index, block):
+        tile = tables[index, block * SUB:(block + 1) * SUB, :]
+        return jnp.concatenate([tile] * (cols // LANES), axis=1)
+
+    def pulled(block):
+        at = slice(block * SUB, (block + 1) * SUB)
+        rate = wide(0, block)
+        for kind in (3, 1):
+            lo, under = kind * layers, (kind // 2) * layers
+            adv[lo:lo + layers, at, :] = adv[lo:lo + layers, at, :] - rate * adv[under:under + layers, at, :]
+
+    def line_of(slab, block):
+        index = ((per_slab - block) % per_slab) * slabs + slab
+        chunk = index // n
+        device = index % n if chunk < chunks - 1 else static_owner(index - n * chunk)
+        return edge_in[chunk, device].reshape(1, 1, LANES)
 
     def static_owner(index):
         if n == 2 * last:
             return 2 * index + (index // 2 + index) % 2
         return (index * n + n - 1) // last
 
-    def ends(slab):
-        sides = ([], [])
-        for block in range(per_slab):
-            index = ((per_slab - block) % per_slab) * slabs + slab
-            chunk = index // n
-            device = index % n if chunk < chunks - 1 else static_owner(index - n * chunk)
-            line = edge_in[device]
-            for side in range(2):
-                spot = jnp.where(small == spots * chunk + SUB * side, line, 0.0)
-                sides[side].append(jnp.sum(spot, axis=1, keepdims=True))
-        return jnp.concatenate(sides[0], axis=0), jnp.concatenate(sides[1], axis=0)
-
-    edges = [ends(slab) for slab in range(slabs)]
-    for slab in range(slabs):
-        here = adv[slab]
-        left, right = edges[slab]
-        if slab // layers in (1, 3):
-            below = slab - layers if slab // layers == 1 else slab - 2 * layers
-            here = here - pull * adv[below]
-            other_left, other_right = edges[below]
-            left = left - pull * other_left
-            right = right - pull * other_right
-        top = jnp.where(inner, halo_in[3, slab:slab + 1, :], 0.0)
-        bottom = jnp.where(outer, halo_in[2, slab:slab + 1, :], 0.0)
-        lower = jnp.where(wide_lane == 0, left, pltpu.roll(here, 1, axis=1))
-        upper = jnp.where(wide_lane == cols - 1, right, pltpu.roll(here, cols - 1, axis=1))
-        above = jnp.where(wide_row == 0, top, pltpu.roll(here, 1, axis=0))
-        beneath = jnp.where(wide_row == rows - 1, bottom, pltpu.roll(here, rows - 1, axis=0))
+    block_row = lax.broadcasted_iota(jnp.int32, (slabs, SUB, cols), 1)
+    block_lane = lax.broadcasted_iota(jnp.int32, (slabs, SUB, cols), 2)
+
+    def diffused(block):
+        low, high = block * SUB, (block + 1) * SUB
+        here = adv[:, low:high, :]
+        own_lines = jnp.concatenate([line_of(slab, block) for slab in range(slabs)], axis=0)
+        none = jnp.zeros((1, 1, LANES), jnp.float32)
+        under = []
+        for slab in range(slabs):
+            kind = slab // layers
+            under.append(line_of(slab - (layers if kind == 1 else 2 * layers), block) if kind in (1, 3) else none)
+        under = jnp.concatenate(under, axis=0)
+        ends = own_lines - tables[0, low:high, :][None] * under
+        left = jnp.sum(jnp.where((small == 0)[None], ends, 0.0), axis=2, keepdims=True)
+        right = jnp.sum(jnp.where((small == SUB)[None], ends, 0.0), axis=2, keepdims=True)
+        if block > 0:
+            top = adv[:, low - 1:low, :]
+        else:
+            top = jnp.where(ring > 0, halo_in[3, :slabs, :], 0.0).reshape(slabs, 1, cols)
+        if block < per_slab - 1:
+            bottom = adv[:, high:high + 1, :]
+        else:
+            bottom = jnp.where(ring < m - 1, halo_in[2, :slabs, :], 0.0).reshape(slabs, 1, cols)
+        lower = jnp.where(block_lane == 0, left, pltpu.roll(here, 1, axis=2))
+        upper = jnp.where(block_lane == cols - 1, right, pltpu.roll(here, cols - 1, axis=2))
+        above = jnp.where(block_row == 0, top, pltpu.roll(here, 1, axis=1))
+        beneath = jnp.where(block_row == SUB - 1, bottom, pltpu.roll(here, SUB - 1, axis=1))
         twice = 2.0 * here
-        out[slab] = (
-            here + along * (lower + upper - twice) + across * (beneath + above - twice)
+        out[:, low:high, :] = (
+            here + wide(1, block)[None] * (lower + upper - twice)
+            + wide(2, block)[None] * (beneath + above - twice)
         )
+
+    def wait_halo():
+        drain(halo_in.at[0], halo_recv.at[0])
+        drain(halo_in.at[1], halo_recv.at[1])
+
+    order = [(per_slab - turn) % per_slab for turn in range(per_slab)]
+    ready, done = set(), set()
+    state = 0
+    for chunk in range(chunks):
+        if chunk < chunks - 1:
+            drain(pieces(n - 1), recv2.at[chunk])
+            drain(lines(n - 1), edge_recv.at[chunk])
+        else:
+            wait_last(pieces, recv2.at[chunk])
+            wait_last(lines, edge_recv.at[chunk])
+        for block in order[len(ready):min(n * (chunk + 1), groups) // slabs]:
+            pulled(block)
+            ready.add(block)
+        if state == 1:
+            wait_halo()
+            state = 2
+        if state == 0 and len(ready) > 1:
+            halo_in[0, :slabs, :] = adv[:, 0:1, :].reshape(slabs, cols)
+            halo_in[1, :slabs, :] = adv[:, rows - 1:rows, :].reshape(slabs, cols)
+            to_rad(halo_in.at[0], halo_in.at[2], halo_send.at[0], halo_recv.at[0], rad_peer(m - 1)).start()
+            to_rad(halo_in.at[1], halo_in.at[3], halo_send.at[1], halo_recv.at[1], rad_peer(1)).start()
+            state = 1
+        if state == 1 and chunk == chunks - 1:
+            wait_halo()
+            state = 2
+        for block in order:
+            near = {block, max(block - 1, 0), min(block + 1, per_slab - 1)}
+            rim = block in (0, per_slab - 1)
+            if block not in done and near <= ready and (state == 2 or not rim):
+                diffused(block)
+                done.add(block)
 
     drain(mass.at[pl.ds(0, n - 1)], mass_send)
     drain(total.at[pl.ds(0, m - 1)], total_send)
-    drain(edge_in.at[pl.ds(0, n - 1)], edge_send)
     drain(halo_in.at[0], halo_send.at[0])
     drain(halo_in.at[1], halo_send.at[1])
 
     def wait_sent(chunk, _):
         drain(pieces(n - 1), send1.at[chunk])
         drain(pieces(n - 1), send2.at[chunk])
+        drain(lines(n - 1), edge_send.at[chunk])
         return 0
 
     lax.fori_loop(0, chunks - 1, wait_sent, 0)
-    wait_last(send1.at[chunks - 1])
+    wait_last(pieces, send1.at[chunks - 1])
 
     @pl.when(held)
     def _():
         drain(pieces(n - 1), send2.at[chunks - 1])
+        drain(lines(n - 1), edge_send.at[chunks - 1])
 
 
 def shards(n, m, fields, shifts, area, gravity, kappa_az, kappa_rad):
@@ -333,7 +363,6 @@
     dma = pltpu.SemaphoreType.DMA
     vmem = pl.BlockSpec(memory_space=pltpu.VMEM)
     hbm = pl.BlockSpec(memory_space=pltpu.HBM)
-    assert 2 * SUB * chunks <= LANES
     slab_pad = -(-slabs // SUB) * SUB
     updated, enclosed = pl.pallas_call(
         functools.partial(kernel, n, m, layers),
@@ -351,18 +380,18 @@
             pltpu.VMEM((chunks, n, SUB, cols), f32),
             pltpu.VMEM((chunks, n, SUB, cols), f32),
             pltpu.VMEM((slabs, rows, cols), f32),
-            pltpu.VMEM((n, SUB, LANES), f32),
-            pltpu.VMEM((n, 1, LANES), f32),
-            pltpu.VMEM((n, 1, LANES), f32),
+            pltpu.VMEM((chunks, n, 1, LANES), f32),
+            pltpu.VMEM((chunks, n, 1, LANES), f32),
             pltpu.VMEM((n, 1, LANES), f32),
             pltpu.VMEM((m, 1, LANES), f32),
             pltpu.VMEM((rows, LANES), jnp.int32),
+            pltpu.VMEM((3, rows, LANES), f32),
             pltpu.VMEM((4, slab_pad, cols), f32),
             dma((chunks,)), dma((chunks,)), dma((chunks,)), dma((chunks,)),
-            dma, dma, dma, dma, dma, dma, dma((2,)), dma((2,)),
+            dma, dma, dma, dma, dma((chunks,)), dma((chunks,)), dma((2,)), dma((2,)),
         ],
         compiler_params=pltpu.CompilerParams(
-            collective_id=0, has_side_effects=True, vmem_limit_bytes=32 * 1024 * 1024
+            collective_id=0, has_side_effects=True, vmem_limit_bytes=105 * 512 * 1024
         ),
     )(
         fields.reshape(slabs, rows, cols), shifts.reshape(line), area.reshape(line),

time: 56.7 us -> 55.9 us (0.986)
  local copies, waits for them, and re-layouts: 3.34 us -> 2.14 us
    unnamed x14 -> x12, local copies, waits for them, and re-layouts: 3.34 us -> 2.14 us
where the time goes in v6:
time: 55.9 us; the launch traced here: 55.8 us
  Pallas kernels  53 us (95%)
  local copies, waits for them, and re-layouts  2.14 us (4%)
  between operations  0.68 us (1%)
    pallas_call x1, Pallas kernels, shards(): pl.pallas_call(functools.partial(kernel, n, m, layers), out_shape=(jax.Sh...  53 us
    unnamed x12, local copies, waits for them, and re-layouts  2.14 us

profile of v6, /device:TPU:0, one launch (start us, length us, event | category | flops | bytes accessed | tf_op | source)
XLA Modules:
  0.0 55.8 jit_solution(629235386884781257)
XLA Ops:
  0.6 0.0 copy-start.3
  0.6 0.0 copy-start.4
  0.7 0.0 copy-start
  0.7 0.0 copy-start.1
  0.7 0.0 copy-start.2
  0.7 0.6 %copy-done.3 = f32[96]{0:T(128)S(1)} copy-done((f32[96]{0:T(128)S(1)}, f32[96]{0:T(128)}, u32[]{:S(2)}) %copy-start.3) | copy-done | bytes 408
  1.3 0.0 copy-done.4
  1.3 0.0 copy-done
  1.3 0.0 copy-done.1
  1.3 0.0 copy-done.2
  1.4 53.0 %shard_map.77 = (f32[10,96,256]{2,1,0:T(8,128)S(1)}, f32[1,96]{1,0:T(1,128)S(1)}) custom-call(f32[10,96,256]{2,1,0:T(8,128)} %bitcast.15, s32[1,96]{1,0:T(1,128)S(1)} %bitcast.9, f32[1,96]{1,0:T(1,128)S(1)} %bitcast.10, f32[1,96]{1,0:T(1,128)S(1)} %bitcast.11, f32[1,96]{1,0:T(1,128)S(1)} %bitcast.12, f32[1,96]{1,0:T(1,128)S(1)} %bitcast.13), custom_call_target="tpu_custom_call" | custom-call | tf_op jit(solution)/shard_map/pallas_call | solution.py:367
  54.3 0.9 %copy.10 = f32[5,2,96,256]{3,2,1,0:T(8,128)} copy(f32[5,2,96,256]{3,2,1,0:T(8,128)S(1)} %bitcast.8) | data formatting | bytes 1966080
  55.3 0.5 copy.11
Async XLA Ops:
  0.6 0.7 %copy-start.3 = (f32[96]{0:T(128)S(1)}, f32[96]{0:T(128)}, u32[]{:S(2)}) copy-start(f32[96]{0:T(128)} %param.10) | copy-start | bytes 1156
  0.6 0.7 %copy-start.4 = (f32[96]{0:T(128)S(1)}, f32[96]{0:T(128)}, u32[]{:S(2)}) copy-start(f32[96]{0:T(128)} %param.11) | copy-start | bytes 1156
  0.7 0.7 %copy-start = (s32[96]{0:T(128)S(1)}, s32[96]{0:T(128)}, u32[]{:S(2)}) copy-start(s32[96]{0:T(128)} %param.7) | copy-start | bytes 1156
  0.7 0.7 %copy-start.1 = (f32[96]{0:T(128)S(1)}, f32[96]{0:T(128)}, u32[]{:S(2)}) copy-start(f32[96]{0:T(128)} %param.8) | copy-start | bytes 1156
  0.7 0.7 %copy-start.2 = (f32[96]{0:T(128)S(1)}, f32[96]{0:T(128)}, u32[]{:S(2)}) copy-start(f32[96]{0:T(128)} %param.9) | copy-start | bytes 1156

commit v7 on v6

--- a/solution.py
+++ b/solution.py
@@ -76,21 +76,21 @@
             (gravity_in, gravity), (kappa_az_in, kappa_az), (kappa_rad_in, kappa_rad),
         ))
     ]
+    barrier = pltpu.get_barrier_semaphore()
+
+    def greet(step, _):
+        pl.semaphore_signal(barrier, inc=1, device_id={"az": peer(step)}, device_id_type=MESH)
+        return 0
+
+    def greet_rad(step, _):
+        pl.semaphore_signal(barrier, inc=1, device_id={"rad": rad_peer(step)}, device_id_type=MESH)
+        return 0
+
+    lax.fori_loop(1, n, greet, 0)
+    lax.fori_loop(1, m, greet_rad, 0)
+
     for load in loads:
         load.start()
-
-    barrier = pltpu.get_barrier_semaphore()
-
-    def greet(step, _):
-        pl.semaphore_signal(barrier, inc=1, device_id={"az": peer(step)}, device_id_type=MESH)
-        return 0
-
-    def greet_rad(step, _):
-        pl.semaphore_signal(barrier, inc=1, device_id={"rad": rad_peer(step)}, device_id_type=MESH)
-        return 0
-
-    lax.fori_loop(1, n, greet, 0)
-    lax.fori_loop(1, m, greet_rad, 0)
 
     row_at = lax.broadcasted_iota(jnp.int32, (rows, LANES), 0)
     lane_at = lax.broadcasted_iota(jnp.int32, (rows, LANES), 1)
@@ -100,21 +100,7 @@
     def as_column(line):
         return jnp.sum(jnp.where(square_row == square_lane, line, 0.0), axis=1, keepdims=True)
 
-    for load in loads:
-        load.wait()
-    density = fields[0]
-    for z in range(1, layers):
-        density = density + fields[z]
-    local = jnp.sum(density, axis=1, keepdims=True)
-    mass[me] = jnp.sum(jnp.where(row_at == lane_at, local, 0.0), axis=0, keepdims=True)
-
     pl.semaphore_wait(barrier, n - 1 + m - 1)
-
-    def send_mass(step, _):
-        to_peer(mass.at[me], mass.at[me], mass_send, mass_recv, peer(step)).start()
-        return 0
-
-    lax.fori_loop(1, n, send_mass, 0)
 
     def send_rows(chunk, _):
         def one(step, _):
@@ -144,6 +130,20 @@
         return 0
 
     lax.fori_loop(1, n, send_last, 0)
+
+    for load in loads:
+        load.wait()
+    density = fields[0]
+    for z in range(1, layers):
+        density = density + fields[z]
+    local = jnp.sum(density, axis=1, keepdims=True)
+    mass[me] = jnp.sum(jnp.where(row_at == lane_at, local, 0.0), axis=0, keepdims=True)
+
+    def send_mass(step, _):
+        to_peer(mass.at[me], mass.at[me], mass_send, mass_recv, peer(step)).start()
+        return 0
+
+    lax.fori_loop(1, n, send_mass, 0)
 
     shift_column = as_column(shifts[...].astype(jnp.float32)).astype(jnp.int32)
     shift_rows = jnp.broadcast_to(shift_column, (rows, LANES))

time: 55.9 us -> 56 us (level)
  no operation moved by 1% of the time
where the time goes in v7:
time: 56 us; the launch traced here: 55.8 us
  Pallas kernels  53 us (95%)
  local copies, waits for them, and re-layouts  2.14 us (4%)
  between operations  0.68 us (1%)
    pallas_call x1, Pallas kernels, shards(): pl.pallas_call(functools.partial(kernel, n, m, layers), out_shape=(jax.Sh...  53 us
    unnamed x12, local copies, waits for them, and re-layouts  2.14 us

profile of v7, /device:TPU:0, one launch (start us, length us, event | category | flops | bytes accessed | tf_op | source)
XLA Modules:
  0.0 55.8 jit_solution(3522885118993835194)
XLA Ops:
  0.6 0.0 copy-start.3
  0.6 0.0 copy-start.4
  0.7 0.0 copy-start
  0.7 0.0 copy-start.1
  0.7 0.0 copy-start.2
  0.7 0.6 %copy-done.3 = f32[96]{0:T(128)S(1)} copy-done((f32[96]{0:T(128)S(1)}, f32[96]{0:T(128)}, u32[]{:S(2)}) %copy-start.3) | copy-done | bytes 408
  1.3 0.0 copy-done.4
  1.3 0.0 copy-done
  1.3 0.0 copy-done.1
  1.3 0.0 copy-done.2
  1.4 53.0 %shard_map.77 = (f32[10,96,256]{2,1,0:T(8,128)S(1)}, f32[1,96]{1,0:T(1,128)S(1)}) custom-call(f32[10,96,256]{2,1,0:T(8,128)} %bitcast.15, s32[1,96]{1,0:T(1,128)S(1)} %bitcast.9, f32[1,96]{1,0:T(1,128)S(1)} %bitcast.10, f32[1,96]{1,0:T(1,128)S(1)} %bitcast.11, f32[1,96]{1,0:T(1,128)S(1)} %bitcast.12, f32[1,96]{1,0:T(1,128)S(1)} %bitcast.13), custom_call_target="tpu_custom_call" | custom-call | tf_op jit(solution)/shard_map/pallas_call | solution.py:367
  54.3 0.9 %copy.10 = f32[5,2,96,256]{3,2,1,0:T(8,128)} copy(f32[5,2,96,256]{3,2,1,0:T(8,128)S(1)} %bitcast.8) | data formatting | bytes 1966080
  55.3 0.5 copy.11
Async XLA Ops:
  0.6 0.7 %copy-start.3 = (f32[96]{0:T(128)S(1)}, f32[96]{0:T(128)}, u32[]{:S(2)}) copy-start(f32[96]{0:T(128)} %param.10) | copy-start | bytes 1156
  0.6 0.7 %copy-start.4 = (f32[96]{0:T(128)S(1)}, f32[96]{0:T(128)}, u32[]{:S(2)}) copy-start(f32[96]{0:T(128)} %param.11) | copy-start | bytes 1156
  0.7 0.7 %copy-start = (s32[96]{0:T(128)S(1)}, s32[96]{0:T(128)}, u32[]{:S(2)}) copy-start(s32[96]{0:T(128)} %param.7) | copy-start | bytes 1156
  0.7 0.7 %copy-start.1 = (f32[96]{0:T(128)S(1)}, f32[96]{0:T(128)}, u32[]{:S(2)}) copy-start(f32[96]{0:T(128)} %param.8) | copy-start | bytes 1156
  0.7 0.7 %copy-start.2 = (f32[96]{0:T(128)S(1)}, f32[96]{0:T(128)}, u32[]{:S(2)}) copy-start(f32[96]{0:T(128)} %param.9) | copy-start | bytes 1156

commit v8 on v7

--- a/solution.py
+++ b/solution.py
@@ -10,6 +10,7 @@
 MESH = pl.DeviceIdType.MESH
 SUB = 8
 LANES = 128
+AHEAD = 4
 star_mass = 1.0
 
 
@@ -31,14 +32,20 @@
     ring = lax.axis_index("rad")
 
     def peer(step):
+        if n & (n - 1) == 0:
+            return (me + step) & (n - 1)
         return lax.rem(me + step, n)
+
+    def over(value, by):
+        return (value * (2 ** 18 // by + 1)) >> 18 if groups < 2 ** 12 and by < 64 else lax.div(value, by)
 
     def rad_peer(step):
         return lax.rem(ring + step, m)
 
     def place(group):
-        slab = lax.rem(group, slabs)
-        block = lax.rem(per_slab - lax.div(group, slabs), per_slab)
+        turn = over(group, slabs)
+        slab = group - turn * slabs
+        block = jnp.where(turn == 0, 0, per_slab - turn)
         return slab, pl.ds(pl.multiple_of(block * SUB, SUB), SUB)
 
     def owner(index):
@@ -113,7 +120,8 @@
 
         return lax.fori_loop(1, n, one, 0)
 
-    lax.fori_loop(0, chunks - 1, send_rows, 0)
+    ahead = min(AHEAD, chunks - 1)
+    lax.fori_loop(0, ahead, send_rows, 0)
 
     def send_last(step, _):
         device = peer(step)
@@ -128,8 +136,6 @@
             ).start()
 
         return 0
-
-    lax.fori_loop(1, n, send_last, 0)
 
     for load in loads:
         load.wait()
@@ -165,14 +171,6 @@
             wout[chunk, i] = row[:, i * cols:(i + 1) * cols]
         adv[slab, block, :] = wout[chunk, me]
 
-        def back(step, _):
-            device = peer(step)
-            to_peer(
-                wout.at[chunk, device], adv.at[slab, block], send2.at[chunk], recv2.at[chunk], device
-            ).start()
-            return 0
-
-        lax.fori_loop(1, n, back, 0)
         for i in range(n):
             low = (i * cols - 1) % cells
             high = (i * cols + cols) % cells
@@ -183,22 +181,31 @@
             edge_out[chunk, i] = jnp.sum(ends, axis=0, keepdims=True)
         edge_in[chunk, me] = edge_out[chunk, me]
 
-        def back_edges(step, _):
+        def back(step, _):
             device = peer(step)
+            to_peer(
+                wout.at[chunk, device], adv.at[slab, block], send2.at[chunk], recv2.at[chunk], device
+            ).start()
             to_peer(
                 edge_out.at[chunk, device], edge_in.at[chunk, me],
                 edge_send.at[chunk], edge_recv.at[chunk], device,
             ).start()
             return 0
 
-        lax.fori_loop(1, n, back_edges, 0)
+        lax.fori_loop(1, n, back, 0)
 
     def turn(chunk, _):
         drain(pieces(n - 1), recv1.at[chunk])
         roll_chunk(chunk, n * chunk + me)
         return 0
 
-    lax.fori_loop(0, chunks - 1, turn, 0)
+    def turn_and_send(chunk, _):
+        turn(chunk, 0)
+        return send_rows(chunk + ahead, 0)
+
+    lax.fori_loop(0, chunks - 1 - ahead, turn_and_send, 0)
+    lax.fori_loop(1, n, send_last, 0)
+    lax.fori_loop(chunks - 1 - ahead, chunks - 1, turn, 0)
     held, group = last_of(me)
 
     @pl.when(held)

time: 56 us -> 54.9 us (0.980)
  Pallas kernels: 53 us -> 51.9 us
    pallas_call x1, Pallas kernels: 53 us -> 51.9 us  [shards(): pl.pallas_call(functools.partial(kernel, n, m, layers), out_shape=(jax.Sh...]
where the time goes in v8:
time: 54.9 us; the launch traced here: 54.7 us
  Pallas kernels  51.9 us (95%)
  local copies, waits for them, and re-layouts  2.14 us (4%)
  between operations  0.68 us (1%)
    pallas_call x1, Pallas kernels, shards(): pl.pallas_call(functools.partial(kernel, n, m, layers), out_shape=(jax.Sh...  51.9 us
    unnamed x12, local copies, waits for them, and re-layouts  2.14 us

profile of v8, /device:TPU:0, one launch (start us, length us, event | category | flops | bytes accessed | tf_op | source)
XLA Modules:
  0.0 54.7 jit_solution(17208109037489727627)
XLA Ops:
  0.6 0.0 copy-start.3
  0.6 0.0 copy-start.4
  0.7 0.0 copy-start
  0.7 0.0 copy-start.1
  0.7 0.0 copy-start.2
  0.7 0.6 %copy-done.3 = f32[96]{0:T(128)S(1)} copy-done((f32[96]{0:T(128)S(1)}, f32[96]{0:T(128)}, u32[]{:S(2)}) %copy-start.3) | copy-done | bytes 408
  1.3 0.0 copy-done.4
  1.3 0.0 copy-done
  1.3 0.0 copy-done.1
  1.3 0.0 copy-done.2
  1.4 51.9 %shard_map.77 = (f32[10,96,256]{2,1,0:T(8,128)S(1)}, f32[1,96]{1,0:T(1,128)S(1)}) custom-call(f32[10,96,256]{2,1,0:T(8,128)} %bitcast.15, s32[1,96]{1,0:T(1,128)S(1)} %bitcast.9, f32[1,96]{1,0:T(1,128)S(1)} %bitcast.10, f32[1,96]{1,0:T(1,128)S(1)} %bitcast.11, f32[1,96]{1,0:T(1,128)S(1)} %bitcast.12, f32[1,96]{1,0:T(1,128)S(1)} %bitcast.13), custom_call_target="tpu_custom_call" | custom-call | tf_op jit(solution)/shard_map/pallas_call | solution.py:374
  53.3 0.9 %copy.10 = f32[5,2,96,256]{3,2,1,0:T(8,128)} copy(f32[5,2,96,256]{3,2,1,0:T(8,128)S(1)} %bitcast.8) | data formatting | bytes 1966080
  54.2 0.5 copy.11
Async XLA Ops:
  0.6 0.7 %copy-start.3 = (f32[96]{0:T(128)S(1)}, f32[96]{0:T(128)}, u32[]{:S(2)}) copy-start(f32[96]{0:T(128)} %param.10) | copy-start | bytes 1156
  0.6 0.7 %copy-start.4 = (f32[96]{0:T(128)S(1)}, f32[96]{0:T(128)}, u32[]{:S(2)}) copy-start(f32[96]{0:T(128)} %param.11) | copy-start | bytes 1156
  0.7 0.7 %copy-start = (s32[96]{0:T(128)S(1)}, s32[96]{0:T(128)}, u32[]{:S(2)}) copy-start(s32[96]{0:T(128)} %param.7) | copy-start | bytes 1156
  0.7 0.7 %copy-start.1 = (f32[96]{0:T(128)S(1)}, f32[96]{0:T(128)}, u32[]{:S(2)}) copy-start(f32[96]{0:T(128)} %param.8) | copy-start | bytes 1156
  0.7 0.7 %copy-start.2 = (f32[96]{0:T(128)S(1)}, f32[96]{0:T(128)}, u32[]{:S(2)}) copy-start(f32[96]{0:T(128)} %param.9) | copy-start | bytes 1156

commit v9 on v8

--- a/solution.py
+++ b/solution.py
@@ -107,6 +107,7 @@
     def as_column(line):
         return jnp.sum(jnp.where(square_row == square_lane, line, 0.0), axis=1, keepdims=True)
 
+    loads[0].wait()
     pl.semaphore_wait(barrier, n - 1 + m - 1)
 
     def send_rows(chunk, _):
@@ -114,7 +115,7 @@
             device = peer(step)
             slab, block = place(n * chunk + device)
             to_peer(
-                source.at[slab, block], win.at[chunk, me], send1.at[chunk], recv1.at[chunk], device
+                fields.at[slab, block], win.at[chunk, me], send1.at[chunk], recv1.at[chunk], device
             ).start()
             return 0
 
@@ -131,13 +132,13 @@
         def _():
             slab, block = place(group)
             to_peer(
-                source.at[slab, block], win.at[chunks - 1, me],
+                fields.at[slab, block], win.at[chunks - 1, me],
                 send1.at[chunks - 1], recv1.at[chunks - 1], device,
             ).start()
 
         return 0
 
-    for load in loads:
+    for load in loads[1:]:
         load.wait()
     density = fields[0]
     for z in range(1, layers):

time: 54.9 us -> 54.7 us (level)
  no operation moved by 1% of the time
where the time goes in v9:
time: 54.7 us; the launch traced here: 54.5 us
  Pallas kernels  51.7 us (95%)
  local copies, waits for them, and re-layouts  2.14 us (4%)
  between operations  0.68 us (1%)
    pallas_call x1, Pallas kernels, shards(): pl.pallas_call(functools.partial(kernel, n, m, layers), out_shape=(jax.Sh...  51.7 us
    unnamed x12, local copies, waits for them, and re-layouts  2.14 us

profile of v9, /device:TPU:0, one launch (start us, length us, event | category | flops | bytes accessed | tf_op | source)
XLA Modules:
  0.0 54.5 jit_solution(11878988722511936297)
XLA Ops:
  0.6 0.0 copy-start.3
  0.6 0.0 copy-start.4
  0.7 0.0 copy-start
  0.7 0.0 copy-start.1
  0.7 0.0 copy-start.2
  0.7 0.6 %copy-done.3 = f32[96]{0:T(128)S(1)} copy-done((f32[96]{0:T(128)S(1)}, f32[96]{0:T(128)}, u32[]{:S(2)}) %copy-start.3) | copy-done | bytes 408
  1.3 0.0 copy-done.4
  1.3 0.0 copy-done
  1.3 0.0 copy-done.1
  1.3 0.0 copy-done.2
  1.4 51.7 %shard_map.77 = (f32[10,96,256]{2,1,0:T(8,128)S(1)}, f32[1,96]{1,0:T(1,128)S(1)}) custom-call(f32[10,96,256]{2,1,0:T(8,128)} %bitcast.15, s32[1,96]{1,0:T(1,128)S(1)} %bitcast.9, f32[1,96]{1,0:T(1,128)S(1)} %bitcast.10, f32[1,96]{1,0:T(1,128)S(1)} %bitcast.11, f32[1,96]{1,0:T(1,128)S(1)} %bitcast.12, f32[1,96]{1,0:T(1,128)S(1)} %bitcast.13), custom_call_target="tpu_custom_call" | custom-call | tf_op jit(solution)/shard_map/pallas_call | solution.py:375
  53.1 0.9 %copy.10 = f32[5,2,96,256]{3,2,1,0:T(8,128)} copy(f32[5,2,96,256]{3,2,1,0:T(8,128)S(1)} %bitcast.8) | data formatting | bytes 1966080
  54.0 0.5 copy.11
Async XLA Ops:
  0.6 0.7 %copy-start.3 = (f32[96]{0:T(128)S(1)}, f32[96]{0:T(128)}, u32[]{:S(2)}) copy-start(f32[96]{0:T(128)} %param.10) | copy-start | bytes 1156
  0.6 0.7 %copy-start.4 = (f32[96]{0:T(128)S(1)}, f32[96]{0:T(128)}, u32[]{:S(2)}) copy-start(f32[96]{0:T(128)} %param.11) | copy-start | bytes 1156
  0.7 0.7 %copy-start = (s32[96]{0:T(128)S(1)}, s32[96]{0:T(128)}, u32[]{:S(2)}) copy-start(s32[96]{0:T(128)} %param.7) | copy-start | bytes 1156
  0.7 0.7 %copy-start.1 = (f32[96]{0:T(128)S(1)}, f32[96]{0:T(128)}, u32[]{:S(2)}) copy-start(f32[96]{0:T(128)} %param.8) | copy-start | bytes 1156
  0.7 0.7 %copy-start.2 = (f32[96]{0:T(128)S(1)}, f32[96]{0:T(128)}, u32[]{:S(2)}) copy-start(f32[96]{0:T(128)} %param.9) | copy-start | bytes 1156

commit v10 on v9

--- a/solution.py
+++ b/solution.py
@@ -33,7 +33,7 @@
 
     def peer(step):
         if n & (n - 1) == 0:
-            return (me + step) & (n - 1)
+            return (me + 5 * step) & (n - 1)
         return lax.rem(me + step, n)
 
     def over(value, by):

time: 54.7 us -> 55.8 us (1.020)
  Pallas kernels: 51.7 us -> 52.8 us
    pallas_call x1, Pallas kernels: 51.7 us -> 52.8 us  [shards(): pl.pallas_call(functools.partial(kernel, n, m, layers), out_shape=(jax.Sh...]
where the time goes in v10:
time: 55.8 us; the launch traced here: 55.6 us
  Pallas kernels  52.8 us (95%)
  local copies, waits for them, and re-layouts  2.14 us (4%)
  between operations  0.68 us (1%)
    pallas_call x1, Pallas kernels, shards(): pl.pallas_call(functools.partial(kernel, n, m, layers), out_shape=(jax.Sh...  52.8 us
    unnamed x12, local copies, waits for them, and re-layouts  2.14 us

profile of v10, /device:TPU:0, one launch (start us, length us, event | category | flops | bytes accessed | tf_op | source)
XLA Modules:
  0.0 55.6 jit_solution(11046493710729208435)
XLA Ops:
  0.6 0.0 copy-start.3
  0.6 0.0 copy-start.4
  0.7 0.0 copy-start
  0.7 0.0 copy-start.1
  0.7 0.0 copy-start.2
  0.7 0.6 %copy-done.3 = f32[96]{0:T(128)S(1)} copy-done((f32[96]{0:T(128)S(1)}, f32[96]{0:T(128)}, u32[]{:S(2)}) %copy-start.3) | copy-done | bytes 408
  1.3 0.0 copy-done.4
  1.3 0.0 copy-done
  1.3 0.0 copy-done.1
  1.3 0.0 copy-done.2
  1.4 52.8 %shard_map.77 = (f32[10,96,256]{2,1,0:T(8,128)S(1)}, f32[1,96]{1,0:T(1,128)S(1)}) custom-call(f32[10,96,256]{2,1,0:T(8,128)} %bitcast.15, s32[1,96]{1,0:T(1,128)S(1)} %bitcast.9, f32[1,96]{1,0:T(1,128)S(1)} %bitcast.10, f32[1,96]{1,0:T(1,128)S(1)} %bitcast.11, f32[1,96]{1,0:T(1,128)S(1)} %bitcast.12, f32[1,96]{1,0:T(1,128)S(1)} %bitcast.13), custom_call_target="tpu_custom_call" | custom-call | tf_op jit(solution)/shard_map/pallas_call | solution.py:375
  54.2 0.9 %copy.10 = f32[5,2,96,256]{3,2,1,0:T(8,128)} copy(f32[5,2,96,256]{3,2,1,0:T(8,128)S(1)} %bitcast.8) | data formatting | bytes 1966080
  55.1 0.5 copy.11
Async XLA Ops:
  0.6 0.7 %copy-start.3 = (f32[96]{0:T(128)S(1)}, f32[96]{0:T(128)}, u32[]{:S(2)}) copy-start(f32[96]{0:T(128)} %param.10) | copy-start | bytes 1156
  0.6 0.7 %copy-start.4 = (f32[96]{0:T(128)S(1)}, f32[96]{0:T(128)}, u32[]{:S(2)}) copy-start(f32[96]{0:T(128)} %param.11) | copy-start | bytes 1156
  0.7 0.7 %copy-start = (s32[96]{0:T(128)S(1)}, s32[96]{0:T(128)}, u32[]{:S(2)}) copy-start(s32[96]{0:T(128)} %param.7) | copy-start | bytes 1156
  0.7 0.7 %copy-start.1 = (f32[96]{0:T(128)S(1)}, f32[96]{0:T(128)}, u32[]{:S(2)}) copy-start(f32[96]{0:T(128)} %param.8) | copy-start | bytes 1156
  0.7 0.7 %copy-start.2 = (f32[96]{0:T(128)S(1)}, f32[96]{0:T(128)}, u32[]{:S(2)}) copy-start(f32[96]{0:T(128)} %param.9) | copy-start | bytes 1156
